TPU v7x, 256 devices: a whole 4x4x8 slice. The times are simulated.
256 devices in a mesh: dp: 8 (over z_hi, y), expert: 8 (over z_lo, core), tensor: 4 (over x).
Axes of the slice: x: 4, y: 4, z: 8 (z_hi: 2, z_lo: 4; z = z_hi * 4 + z_lo), core: 2. Of those that a mesh axis runs over, the one named last changes fastest.
Arguments:
- tokens: bfloat16 [1024, 6144], P(('dp', 'expert', 'tensor')), may hold values from -6 to 6
- out_grad: bfloat16 [1024, 6144], P(('dp', 'expert', 'tensor')), may hold values from -6 to 6
- routes: int32 [1024, 2], P(('dp', 'expert', 'tensor')), may hold values from 0 to 7, all different within a row; in each aligned block of 4 rows (0 to 3, 4 to 7, ...) at most 2 rows name the same one
- tasks: int32 [1024], P(('dp', 'expert', 'tensor')), may hold values from 0 to 3
- route_probs: float32 [1024, 2], P(('dp', 'expert', 'tensor')), may hold values from 0.2 to 1
- gate_matrix_frozen: bfloat16 [8, 6144, 8192], P('expert', None, ('dp', 'tensor')), may hold values from -0.078125 to 0.078125
- w_up: bfloat16 [8, 6144, 8192], P('expert', None, ('dp', 'tensor')), may hold values from -0.078125 to 0.078125
- down_matrix: bfloat16 [8, 8192, 6144], P('expert', ('dp', 'tensor')), may hold values from -0.0625 to 0.0625
- gate_down: bfloat16 [8, 6144, 64], P('expert'), may hold values from -0.078125 to 0.078125
- gate_adapter_right: bfloat16 [8, 64, 8192], P('expert', None, ('dp', 'tensor')), may hold values from -1.5 to 1.5
- down_adapter_left: bfloat16 [8, 8192, 64], P('expert', ('dp', 'tensor')), may hold values from -0.0625 to 0.0625
- down_adapter_right: bfloat16 [8, 64, 6144], P('expert'), may hold values from -1.5 to 1.5
Outputs:
- mixed: bfloat16 [1024, 6144], P(('dp', 'expert', 'tensor'))
- grad_gate_down: bfloat16 [8, 6144, 64], P('expert')
- grad_gate_lift: bfloat16 [8, 64, 8192], P('expert', None, ('dp', 'tensor'))
- grad_down_down: bfloat16 [8, 8192, 64], P('expert', ('dp', 'tensor'))
- grad_down_lift: bfloat16 [8, 64, 6144], P('expert')
Inputs may be any that keep to these rules, and one draw needn't show every extreme that they name: `routes`: within the rows of one device no expert is named by more than 2 rows.
All inputs are finite; a program needn't handle non-finite values.
Results may differ from a plain program's by a relative error of at most 0.0066.
Values may be sent and summed in bfloat16 or wider, within the bound.
A program may use at most 128 MiB of HBM per device.

v0:
```python
import jax
import jax.numpy as jnp
from jax import lax
from jax.sharding import PartitionSpec as P

RANK = 16
CAP = 2


adapter_scale = 0.5


def local(
    tokens,
    out_grad,
    routes,
    tasks,
    route_probs,
    gate_matrix_frozen,
    w_up,
    down_matrix,
    gate_down,
    gate_adapter_right,
    down_adapter_left,
    down_adapter_right,
):
    experts = lax.axis_size("expert")
    blocks = lax.axis_size(("dp", "tensor"))
    tok_rows = tokens.shape[0]
    width = tokens.shape[1]
    slots = experts * CAP
    flat_expert = routes.reshape(-1)
    hits = (flat_expert[:, None] == jnp.arange(experts, dtype=jnp.int32)[None, :]).astype(jnp.int32)
    before = jnp.cumsum(hits, axis=0) - hits
    column = flat_expert * CAP + jnp.sum(before * hits, axis=1)
    placed = (column[:, None] == jnp.arange(slots, dtype=jnp.int32)[None, :]).astype(jnp.float32)
    placed_pairs = placed.reshape(tok_rows, 2, slots)
    selector = jnp.sum(placed_pairs, axis=1).astype(jnp.bfloat16)
    combine = jnp.sum(placed_pairs * route_probs[:, :, None], axis=1)
    dout_pairs = (route_probs[:, :, None] * out_grad.astype(jnp.float32)[:, None, :]).astype(
        jnp.bfloat16
    )
    send_x = jnp.dot(selector.T, tokens, preferred_element_type=jnp.float32).astype(jnp.bfloat16)
    send_dout = jnp.dot(
        placed.astype(jnp.bfloat16).T,
        dout_pairs.reshape(2 * tok_rows, width),
        preferred_element_type=jnp.float32,
    ).astype(jnp.bfloat16)
    send_task = jnp.dot(tasks.astype(jnp.float32)[None, :], selector.astype(jnp.float32))[0].astype(
        jnp.bfloat16
    )
    moved_x, moved_dout, moved_task = (
        lax.all_to_all(
            send_x.reshape(experts, CAP, width), "expert", split_axis=0, concat_axis=0, tiled=True
        ),
        lax.all_to_all(
            send_dout.reshape(experts, CAP, width),
            "expert",
            split_axis=0,
            concat_axis=0,
            tiled=True,
        ),
        lax.all_to_all(
            send_task.reshape(experts, CAP), "expert", split_axis=0, concat_axis=0, tiled=True
        ),
    )
    input_rows, gradient_rows, rows_task = (
        lax.all_gather(moved_x.reshape(slots, width), ("dp", "tensor"), axis=0, tiled=True),
        lax.all_gather(moved_dout.reshape(slots, width), ("dp", "tensor"), axis=0, tiled=True),
        lax.all_gather(moved_task.reshape(slots), ("dp", "tensor"), axis=0, tiled=True),
    )
    gate_matrix = gate_matrix_frozen[0]
    up_w = w_up[0]
    down_w = down_matrix[0]
    first_gate = gate_down[0]
    second_gate = gate_adapter_right[0]
    down_left_factor = down_adapter_left[0]
    down_right_factor = down_adapter_right[0]
    columns = first_gate.shape[1]
    bands = (jnp.arange(columns, dtype=jnp.int32) // RANK).astype(jnp.float32)
    mask = rows_task.astype(jnp.float32)[:, None] == bands[None, :]
    gate_lowrank = jnp.where(
        mask, jnp.dot(input_rows, first_gate, preferred_element_type=jnp.float32), 0.0
    ).astype(jnp.bfloat16)
    gate_activation = jnp.dot(
        input_rows, gate_matrix, preferred_element_type=jnp.float32
    ) + adapter_scale * jnp.dot(gate_lowrank, second_gate, preferred_element_type=jnp.float32)
    upval = jnp.dot(input_rows, up_w, preferred_element_type=jnp.float32)
    hidden_state = (jax.nn.silu(gate_activation) * upval).astype(jnp.bfloat16)
    z_part = jnp.where(
        mask, jnp.dot(hidden_state, down_left_factor, preferred_element_type=jnp.float32), 0.0
    )
    latent_lowrank = lax.psum(z_part, ("dp", "tensor")).astype(jnp.bfloat16)
    own_rows = hidden_state.shape[0] // blocks
    reduced_total = lax.psum_scatter(
        jnp.dot(hidden_state, down_w, preferred_element_type=jnp.float32),
        ("dp", "tensor"),
        scatter_dimension=0,
        tiled=True,
    )
    owned_rows = lax.dynamic_slice_in_dim(
        latent_lowrank, lax.axis_index(("dp", "tensor")) * own_rows, own_rows, 0
    )
    reduced_total = reduced_total + adapter_scale * jnp.dot(
        owned_rows, down_right_factor, preferred_element_type=jnp.float32
    )
    returned = lax.all_to_all(
        reduced_total.reshape(experts, CAP, width),
        "expert",
        split_axis=0,
        concat_axis=0,
        tiled=True,
    )
    mixed = jnp.dot(
        combine, returned.reshape(slots, width), precision=lax.Precision.HIGHEST
    ).astype(jnp.bfloat16)
    combined_lowrank = jnp.where(
        mask, jnp.dot(gradient_rows, down_right_factor.T, preferred_element_type=jnp.float32), 0.0
    ).astype(jnp.bfloat16)
    hidden_gradient = jnp.dot(
        gradient_rows, down_w.T, preferred_element_type=jnp.float32
    ) + adapter_scale * jnp.dot(
        combined_lowrank, down_left_factor.T, preferred_element_type=jnp.float32
    )
    sig = jax.nn.sigmoid(gate_activation)
    gate_gradient = (hidden_gradient * upval * sig * (1.0 + gate_activation * (1.0 - sig))).astype(
        jnp.bfloat16
    )
    expert_portion = jnp.where(
        mask, jnp.dot(gate_gradient, second_gate.T, preferred_element_type=jnp.float32), 0.0
    )
    hidden_rows = input_rows.astype(jnp.float32)
    shard_gradient = adapter_scale * jnp.dot(
        hidden_rows.T, expert_portion, precision=lax.Precision.HIGHEST
    )
    grad_first_gate = lax.psum(shard_gradient, ("dp", "tensor"))
    gate_right_gradient = adapter_scale * jnp.dot(
        gate_lowrank.T, gate_gradient, preferred_element_type=jnp.float32
    )
    down_left_gradient = adapter_scale * jnp.dot(
        hidden_state.T, combined_lowrank, preferred_element_type=jnp.float32
    )
    down_right_gradient = adapter_scale * jnp.dot(
        latent_lowrank.T, gradient_rows, preferred_element_type=jnp.float32
    )
    return (
        mixed,
        grad_first_gate.astype(jnp.bfloat16)[None],
        gate_right_gradient.astype(jnp.bfloat16)[None],
        down_left_gradient.astype(jnp.bfloat16)[None],
        down_right_gradient.astype(jnp.bfloat16)[None],
    )


def solution(mesh):
    return jax.shard_map(
        local,
        mesh=mesh,
        in_specs=(
            P(("dp", "expert", "tensor"), None),
            P(("dp", "expert", "tensor"), None),
            P(("dp", "expert", "tensor"), None),
            P(("dp", "expert", "tensor")),
            P(("dp", "expert", "tensor"), None),
            P("expert", None, ("dp", "tensor")),
            P("expert", None, ("dp", "tensor")),
            P("expert", ("dp", "tensor"), None),
            P("expert", None, None),
            P("expert", None, ("dp", "tensor")),
            P("expert", ("dp", "tensor"), None),
            P("expert", None, None),
        ),
        out_specs=(
            P(("dp", "expert", "tensor"), None),
            P("expert", None, None),
            P("expert", None, ("dp", "tensor")),
            P("expert", ("dp", "tensor"), None),
            P("expert", None, None),
        ),
        check_vma=False,
    )
```

profile of v0, /device:TPU:1, one launch (start us, length us, event | category | flops | bytes accessed | tf_op | source)
XLA Modules:
  0.0 644.2 jit_solution(16520557508530781438)
XLA Ops:
  7.2 0.0 copy-start
  7.2 0.0 all-gather.3.cloned.1.call-start
  7.2 0.9 copy.30
  8.1 0.1 eq.48
  8.2 0.1 fusion.33
  8.3 0.2 select_reduce_fusion.1
  8.5 0.5 copy-done.8
  9.0 0.1 reduce_sum.30
  9.1 0.1 copy.32
  9.2 0.8 convert_reduce_fusion
  10.0 1.0 convolution_convert_fusion.1
  11.0 0.1 reshape.91
  11.2 13.7 %all_to_all.21 = bf16[8,2,6144]{2,1,0:T(2,128)(2,1)S(1)} all-to-all(bf16[8,2,6144]{2,1,0:T(2,128)(2,1)S(1)} %reshape.91), channel_id=1, replica_groups=mesh['dp'=8,'expert'=8,'tensor'=4] {'expert'}, dimensions={0} | all-to-all | bytes 393216 | tf_op jit(solution)/shard_map/all_to_all | solution.py:53
  24.8 0.8 reshape.92
  25.6 0.0 all-gather.3.cloned.1.call-update
  25.6 0.0 all-gather.5.cloned.1.call-start
  25.7 0.8 copy.34
  26.4 0.1 mul.112
  26.5 0.9 mul.114
  27.4 0.1 mul.115
  27.5 0.7 multiply_add_fusion.1
  28.2 0.3 convolution_convert_fusion
  28.5 0.1 reshape.96
  28.7 10.7 %all_to_all.22 = bf16[8,2,6144]{2,1,0:T(2,128)(2,1)S(1)} all-to-all(bf16[8,2,6144]{2,1,0:T(2,128)(2,1)S(1)} %reshape.96), channel_id=1, replica_groups=mesh['dp'=8,'expert'=8,'tensor'=4] {'expert'}, dimensions={0} | all-to-all | bytes 393216 | tf_op jit(solution)/shard_map/all_to_all | solution.py:56
  39.4 0.8 reshape.97
  40.2 0.0 all-gather.5.cloned.1.call-update
  40.2 0.8 fusion.23
  41.0 0.7 convert_element_type.111
  41.6 5.1 all-to-all-start.1
  46.7 1.3 dynamic-slice
  48.7 2.9 all-to-all-done.1
  51.6 0.1 reshape.98
  51.7 0.2 dynamic-update-slice
  51.9 113.2 %all-reduce = bf16[512]{0:T(512)(128)(2,1)S(1)} all-reduce(bf16[512]{0:T(512)(128)(2,1)S(1)} %dynamic-update-slice), channel_id=1, replica_groups=mesh['dp'=8,'expert'=8,'tensor'=4] {'dp','tensor'}, use_global_device_ids=true, to_apply=%add | all-reduce | flops 512 | bytes 2048
  165.1 0.0 all-gather.3.cloned.1.call-done
  165.1 5.1 fusion.17
  170.3 0.0 copy-start.5
  170.3 0.0 copy-start.9
  170.3 3.9 fusion.9
  174.3 0.2 fusion.11
  174.5 2.6 multiply_convert_fusion
  177.1 6.3 fusion.5
  183.5 0.0 reduce-scatter.2.cloned.1.call-update
  183.5 106.6 %all-gather.5.cloned.1.call-done = bf16[512,6144]{1,0:T(8,128)(2,1)} async-done(((bf16[16,6144]{1,0:T(8,128)(2,1)}), bf16[512,6144]{1,0:T(8,128)(2,1)}) %all-gather.5.cloned.1.call-update) | async-done | bytes 6291472 | tf_op jit(solution)/shard_map/all_gather | solution.py:69
  290.0 5.1 fusion.18
  295.2 0.0 copy-start.7
  295.2 0.0 copy-start.10
  295.2 4.8 fusion.3
  300.0 0.4 fusion.16
  300.4 0.7 copy-done.2
  301.1 0.2 convolution_select_fusion.2
  301.3 4.7 convolution_multiply_fusion.1
  306.1 0.9 convolution_select_fusion.3
  306.9 243.8 %all-reduce.3 = (bf16[512,64]{0,1:T(8,128)(2,1)}, bf16[6144,64]{0,1:T(8,128)(2,1)}) all-reduce(f32[512,64]{0,1:T(8,128)} %convolution_select_fusion.3, f32[6144,64]{0,1:T(8,128)} %convolution_multiply_fusion.1), channel_id=1, replica_groups=mesh['dp'=8,'expert'=8,'tensor'=4] {'dp','tensor'}, use_global_device_ids=true, to_apply=%region_5.6 | all-reduce | flops 425984 | bytes 2555904 | tf_op jit(solution)/shard_map/psum | solution.py:93
  550.7 62.4 %reduce-scatter.2.cloned.1.call-done = f32[16,6144]{1,0:T(8,128)} async-done(((f32[512,6144]{1,0:T(8,128)}), f32[16,6144]{1,0:T(8,128)}) %reduce-scatter.2.cloned.1.call-update) | async-done | bytes 393232 | tf_op jit(solution)/shard_map/reduce_scatter | solution.py:95
  613.1 2.3 fusion.2
  615.5 2.0 reshape.94
  617.5 6.2 all-to-all-start.2
  623.6 0.8 fusion.21
  624.4 1.7 fusion.22
  626.2 4.9 fusion.1
  631.1 4.4 all-to-all-done.2
  635.5 1.3 reshape.95
  636.7 0.9 convolution_convert_fusion.2
  (27 shorter events, 0.1 us)
Async XLA Ops:
  7.2 170.0 %copy-start = (bf16[1,256,6144]{2,1,0:T(8,128)(2,1)S(1)}, bf16[1,256,6144]{2,1,0:T(8,128)(2,1)}, u32[]{:S(2)}) copy-start(bf16[1,256,6144]{2,1,0:T(8,128)(2,1)} %param.19) | copy-start | bytes 9437188
  7.2 157.9 %all-gather.3.cloned.1.call-start = ((), (), s32[]{:S(2)}) async-start(), calls=%async_computation.5 | async-start | bytes 6488064 | tf_op jit(solution)/shard_map/all_gather | solution.py:68
  8.5 0.5 copy-start.8
  25.6 264.4 %all-gather.5.cloned.1.call-start = ((), (), s32[]{:S(2)}) async-start(), calls=%async_computation.7 | async-start | bytes 6488064 | tf_op jit(solution)/shard_map/all_gather | solution.py:69
  41.6 9.9 %all-to-all-start.1 = ((bf16[8,1,2]{2,1,0:T(2,128)(2,1)}), bf16[8,1,2]{2,1,0:T(2,128)(2,1)S(1)}, u32[]{:S(2)}, u32[]{:S(2)}) async-start(bf16[8,1,2]{2,1,0:T(2,128)(2,1)} %convert_element_type.111), calls=%async_computation.1 | async-start | bytes 8192 | tf_op jit(solution)/shard_map/all_to_all | solution.py:63
  46.7 566.4 %reduce-scatter.2.cloned.1.call-start = ((), (), s32[]{:S(2)}) async-start(), calls=%async_computation.6 | async-start | bytes 12976128 | tf_op jit(solution)/shard_map/reduce_scatter | solution.py:95
  165.1 5.1 copy-start.1
  170.3 4.0 copy-start.5
  170.3 4.2 copy-start.9
  174.5 2.6 copy-start.3
  290.0 11.3 %slice-start = ((s8[6291456]{0:T(1024)(128)(4,1)}), s8[4194304]{0:T(1024)(128)(4,1)S(1)}, s32[]{:S(2)}) async-start(s8[6291456]{0:T(1024)(128)(4,1)} %bitcast.71), calls=%async_computation.8 | async-start | bytes 8388608
  295.2 4.8 copy-start.4
  295.2 4.8 copy-start.7
  295.2 4.8 copy-start.10
  295.2 5.9 copy-start.6
  295.2 6.1 slice-start.1
  300.4 0.7 copy-start.2
  617.5 18.0 %all-to-all-start.2 = ((f32[8,2,6144]{2,1,0:T(2,128)}), f32[8,2,6144]{2,1,0:T(2,128)}, u32[]{:S(2)}, u32[]{:S(2)}) async-start(f32[8,2,6144]{2,1,0:T(2,128)} %reshape.94), calls=%async_computation.3 | async-start | bytes 786432 | tf_op jit(solution)/shard_map/all_to_all | solution.py:107
Sparse Core Ops, SparseCore 0:
  25.7 133.4 all-gather.2
  162.7 127.2 all-gather.4
  295.8 317.3 reduce-scatter.1
where the time goes:
time: 645 us; the launch traced here: 644 us
  blocking collectives  381 us (59%)
  waiting for transfers between devices  176 us (27%)
  matrix products  47.1 us (7%)
  between operations  14.7 us (2%)
  local copies, waits for them, and re-layouts  11.6 us (2%)
  starting transfers between devices  11.4 us (2%)
    psum x1, blocking collectives, local(): latent_lowrank = lax.psum(z_part, ('dp', 'tensor')).astype(jnp.bfloat16)  244 us
    unnamed x1, blocking collectives  113 us
    all_gather x1, waiting for transfers between devices, local(): lax.all_gather(moved_dout.reshape(slots, width), ('dp', 'tensor'), axis=0...  107 us
    reduce_scatter x1, waiting for transfers between devices, local(): lax.psum_scatter(jnp.dot(hidden_state, down_w, preferred_element_type=jnp...  62.4 us
    all_to_all x1, blocking collectives, local(): lax.all_to_all(send_x.reshape(experts, CAP, width), 'expert', split_axis=...  13.7 us
  transfers between devices with their start and end apart: 5, of which 4 were waited for; matrix products, arithmetic and copies ran while one was open for 8% of the time, Pallas kernels for 0%

commit v1 on v0

v1 whole, which is shorter than its diff:
```python
import functools

import jax
import jax.numpy as jnp
from jax import lax
from jax.experimental import pallas as pl
from jax.experimental.pallas import tpu as pltpu
from jax.sharding import PartitionSpec as P

RANK = 16
SCALE = 0.5
MESH = pl.DeviceIdType.MESH
BF = jnp.bfloat16
F32 = jnp.float32
WIDTH = 512
TILE = 256
MAX_COPIES = 400

RS_PHASES = (
    (("x", 4, (4, 8, 16, 512), (2, 8, 16, 512)), ("y", 4, (8, 16, 512), (4, 16, 512)), ("z", 8, (16, 512), None)),
    (("y", 4, (4, 8, 16, 512), (2, 8, 16, 512)), ("z", 8, (4, 16, 512), (2, 16, 512)), ("x", 4, (16, 512), None)),
    (("z", 8, (4, 4, 16, 512), (2, 4, 16, 512)), ("x", 4, (4, 16, 512), (2, 16, 512)), ("y", 4, (16, 512), None)),
)


def rs_buffers():
    shapes = {}
    for k, phases in enumerate(RS_PHASES):
        for p, (_, n, block, half) in enumerate(phases):
            for way in range(2):
                for slot in range(n // 2):
                    shape = block
                    if slot == 0:
                        if half is None and way == 1:
                            continue
                        shape = half or block
                    shapes[("rs", k, p, way, slot)] = pltpu.VMEM(shape, BF)
    return shapes


def scratch():
    shapes = {
        "X": pltpu.VMEM((6, 4, 4, 8, 16, WIDTH), BF),
        "G": pltpu.VMEM((6, 4, 4, 8, 16, WIDTH), BF),
        "OUT": pltpu.VMEM((3, 4, 4, 8, 16, WIDTH), BF),
        "STAGE": pltpu.VMEM((3, 2, 4, 8, 16, WIDTH), BF),
        "SIB": pltpu.VMEM((3, 4, 4, 8, 16, WIDTH), BF),
        "DOWN": pltpu.VMEM((256, 6144), BF),
        "W": pltpu.VMEM((2, 2, WIDTH, 256), BF),
        "G1T": pltpu.VMEM((64, 6144), BF),
        "L2": pltpu.VMEM((64, 6144), BF),
        "ACC": pltpu.VMEM((1024, 512), F32),
        "A64": pltpu.VMEM((1024, 64), F32),
        "H": pltpu.VMEM((1024, 256), F32),
        "MK": pltpu.VMEM((1024, 128), F32),
        "PB": pltpu.VMEM((1024, 128), F32),
        "ZP": pltpu.VMEM((1024, 64), F32),
        "HID": pltpu.VMEM((1024, 256), BF),
        "DG": pltpu.VMEM((1024, 256), BF),
        "A": pltpu.VMEM((1024, 64), BF),
        "ZS": pltpu.VMEM((1024, 64), BF),
        "C": pltpu.VMEM((1024, 64), BF),
        "T32": pltpu.VMEM((2, 4, 4, 1536), F32),
        "M32": pltpu.VMEM((4, 128), F32),
        "R": pltpu.VMEM((2, 4, 4, 1536), F32),
        "MR": pltpu.VMEM((4, 4, 128), F32),
        "F": pltpu.VMEM((2, 16, 1536), F32),
        "FM": pltpu.VMEM((16, 128), F32),
        "MZ": pltpu.VMEM((8, 16, 128), BF),
        "MF": pltpu.VMEM((2, 4, 16, 128), BF),
        "ZR": pltpu.VMEM((4, 32, 256), F32),
        "AX": pltpu.VMEM((4, 32, 256), F32),
        "YS": pltpu.VMEM((4, 8, 256), F32),
        "AY": pltpu.VMEM((4, 8, 256), F32),
        "HS": pltpu.VMEM((8, 256), F32),
        "HR": pltpu.VMEM((8, 256), F32),
        "FY": pltpu.VMEM((4, 8, 256), F32),
        "FX": pltpu.VMEM((4, 4, 8, 256), F32),
        "LZ": pltpu.VMEM((64, 1024), BF),
        "LR": pltpu.VMEM((128, 1024), BF),
        "S32": pltpu.VMEM((4, 4, 1536), F32),
        "MX": pltpu.VMEM((4, 4, 1536), F32),
        "send": pltpu.SemaphoreType.DMA((MAX_COPIES,)),
        "recv": pltpu.SemaphoreType.DMA((MAX_COPIES,)),
        "local": pltpu.SemaphoreType.DMA((8,)),
    }
    shapes.update(rs_buffers())
    return shapes


def dot(a, b, ca=1, cb=0):
    return lax.dot_general(a, b, (((ca,), (cb,)), ((), ())), preferred_element_type=F32)


def body(names, tok, og, meta, wg, wu, down, g1t, l1, g2t, l2, mixed, o_gd, o_gl, o_dd, o_dl, *refs):
    s = dict(zip(names, refs))
    X, G, OUT, SIB = s["X"], s["G"], s["OUT"], s["SIB"]
    dp, ex, x = lax.axis_index("dp"), lax.axis_index("expert"), lax.axis_index("tensor")
    h, y = dp // 4, dp % 4
    zl, c = ex // 2, ex % 2
    z = h * 4 + zl
    xlo, xhi = x % 2, x // 2
    xp = xlo * 2 + xhi
    grp = xlo * 2 + c

    def device(x_, y_, z_, c_):
        return ((z_ // 4) * 4 + y_, (z_ % 4) * 2 + c_, x_)

    def around(v, d, n):
        return lax.rem(v + (d + n), n)

    def xperm(i):
        return lax.rem(i, 2) * 2 + i // 2

    xdev = [device(around(x, d, 4), y, z, c) for d in range(4)]
    ydev = [device(x, around(y, d, 4), z, c) for d in range(4)]
    zdev = {1: device(x, y, around(z, 1, 8), c), -1: device(x, y, around(z, -1, 8), c)}
    far = device(x, y, around(z, 4, 8), c)
    sibling = device(x, y, z, 1 - c)
    xpair = xhi * 2 + (1 - xlo)
    pair = device(xpair, y, z, c)
    pair_sibling = device(xpair, y, z, 1 - c)
    steps = {"x": (x, 4, xdev[1], xdev[3]), "y": (y, 4, ydev[1], ydev[3]), "z": (z, 8, zdev[1], zdev[-1])}

    count = [0]
    pending = []

    def send(src, dst, target):
        i = count[0]
        count[0] += 1
        copy = pltpu.make_async_remote_copy(
            src_ref=src, dst_ref=dst, send_sem=s["send"].at[i], recv_sem=s["recv"].at[i],
            device_id=target, device_id_type=MESH,
        )
        copy.start()
        pending.append(copy)
        return copy

    local_down = pltpu.make_async_copy(down, s["DOWN"], s["local"].at[0])
    local_g1 = pltpu.make_async_copy(g1t, s["G1T"], s["local"].at[1])
    local_l2 = pltpu.make_async_copy(l2, s["L2"], s["local"].at[2])

    def weight_copies(j):
        b = order_b[j]
        rows = pl.ds(pl.multiple_of(b * WIDTH, WIDTH), WIDTH)
        slot = j % 2
        return (
            pltpu.make_async_copy(wg.at[rows, :], s["W"].at[slot, 0], s["local"].at[3 + 2 * slot]),
            pltpu.make_async_copy(wu.at[rows, :], s["W"].at[slot, 1], s["local"].at[4 + 2 * slot]),
        )

    use = [(cc, k, lo) for k in (0, 1, 2) for cc in (0, 1) for lo in (0, 1)]
    half_of = (c, 1 - c)
    order_b = [lo * 6 + half_of[cc] * 3 + k for cc, k, lo in use]

    barrier = pltpu.get_barrier_semaphore()
    greeted = xdev[1:] + ydev[1:] + [zdev[1], zdev[-1], far, sibling, pair_sibling]
    for target in greeted:
        pl.semaphore_signal(barrier, inc=1, device_id=target, device_id_type=MESH)
    local_down.start()
    local_g1.start()
    local_l2.start()
    for j in (0, 1):
        for copy in weight_copies(j):
            copy.start()
    for q in range(4):
        s["T32"][0, q] = tok[:, q * 1536:(q + 1) * 1536].astype(F32)
        s["T32"][1, q] = og[:, q * 1536:(q + 1) * 1536].astype(F32)
    s["M32"][...] = meta[...].astype(F32)
    pl.semaphore_wait(barrier, len(greeted))

    mates = ((xlo * 2 + 1 - c, sibling), ((1 - xlo) * 2 + c, pair), ((1 - xlo) * 2 + 1 - c, pair_sibling))
    first = {}
    for a in range(2):
        first[a] = [send(s["T32"].at[a, g], s["R"].at[a, grp], d) for g, d in mates]
        if a == 0:
            first["m"] = [send(s["M32"], s["MR"].at[grp], d) for g, d in mates]
    s["R"][0, grp] = s["T32"][0, grp]
    s["R"][1, grp] = s["T32"][1, grp]
    s["MR"][grp] = s["M32"][...]

    def own_block(a, buf):
        for copy in first[a]:
            copy.wait_recv()
        for q in range(4):
            s["F"][a, q * 4:q * 4 + 4, :] = s["R"][a, q]
        for k in range(3):
            buf[c * 3 + k, xp, y, z] = s["F"][a, :, k * WIDTH:(k + 1) * WIDTH].astype(BF)

    def all_gather(n, me, plus, minus, blk, half, arrived):
        up, dn = send(blk(me), blk(me), plus), send(blk(me), blk(me), minus)
        arrived(blk(me))
        yield
        reach = n // 2
        for d in range(1, reach):
            last = d == reach - 1
            a, b = around(me, -d, n), around(me, d, n)
            up.wait_recv()
            if not last:
                up = send(blk(a), blk(a), plus)
            elif half is None:
                up = send(blk(a), blk(a), plus)
            else:
                up = send(half(a, 0), half(a, 0), plus)
            arrived(blk(a))
            dn.wait_recv()
            if not last:
                dn = send(blk(b), blk(b), minus)
            elif half is not None:
                dn = send(half(b, 1), half(b, 1), minus)
            arrived(blk(b))
            yield
        opposite = around(me, reach, n)
        up.wait_recv()
        if half is None:
            arrived(blk(opposite))
        else:
            arrived(half(opposite, 0))
            dn.wait_recv()
            arrived(half(opposite, 1))

    def gather_colour(k, buf, forwards):
        ck = c * 3 + k
        if k == 0:
            phases = (
                ("z", lambda i: buf.at[ck, xp, y, i], None),
                ("y", lambda i: buf.at[ck, xp, i], lambda i, g: buf.at[ck, xp, i, pl.ds(4 * g, 4)]),
                ("x", lambda i: buf.at[ck, xperm(i)], lambda i, g: buf.at[ck, xperm(i), pl.ds(2 * g, 2)]),
            )
        elif k == 1:
            phases = (
                ("x", lambda i: buf.at[ck, xperm(i), y, z], None),
                ("z", lambda i: buf.at[ck, :, y, i], lambda i, g: buf.at[ck, pl.ds(2 * g, 2), y, i]),
                ("y", lambda i: buf.at[ck, :, i], lambda i, g: buf.at[ck, pl.ds(2 * g, 2), i]),
            )
        else:
            phases = (
                ("y", lambda i: buf.at[ck, xp, i, z], None),
                ("x", lambda i: buf.at[ck, xperm(i), :, z], lambda i, g: buf.at[ck, xperm(i), pl.ds(2 * g, 2), z]),
                ("z", lambda i: buf.at[ck, :, :, i], lambda i, g: buf.at[ck, pl.ds(2 * g, 2), :, i]),
            )
        for p, (axis, blk, half) in enumerate(phases):
            me, n, plus, minus = steps[axis]
            if p == 2:
                arrived = lambda ref: forwards.append(send(ref, ref, sibling))
            else:
                arrived = lambda ref: None
            yield from all_gather(n, me, plus, minus, blk, half, arrived)

    def gather_meta():
        for copy in first["m"]:
            copy.wait_recv()
        for q in range(4):
            s["FM"][q * 4:q * 4 + 4, :] = s["MR"][q]
        s["MZ"][z] = pltpu.roll(s["FM"][...], z * 16, 1).astype(BF)
        yield from all_gather(8, z, zdev[1], zdev[-1], lambda i: s["MZ"].at[i], None, lambda ref: None)
        total = s["MZ"][0].astype(F32)
        for i in range(1, 8):
            total = total + s["MZ"][i].astype(F32)
        s["MF"][xhi, y] = total.astype(BF)
        yield from all_gather(4, y, ydev[1], ydev[3], lambda i: s["MF"].at[xhi, i], None, lambda ref: None)
        ref = s["MF"].at[xhi]
        plus, minus = send(ref, s["MF"].at[xhi], xdev[2]), None
        yield
        plus.wait_recv()

    def pump(gens, times=1):
        for _ in range(times):
            for gen in list(gens):
                try:
                    next(gen)
                except StopIteration:
                    gens.remove(gen)

    own_block(0, X)
    fx, fg = [], []
    xgens = [gather_colour(2, X, fx), gather_colour(1, X, fx), gather_colour(0, X, fx), gather_meta()]
    pump(xgens, 1)
    own_block(1, G)
    pump(xgens, 4)
    ggens = [gather_colour(2, G, fg), gather_colour(1, G, fg), gather_colour(0, G, fg)]
    while xgens:
        pump(xgens, 1)
        pump(ggens, 1)

    fields = s["MF"][...].astype(F32).reshape(128, 128)
    me_f = ex.astype(F32)
    band = (lax.broadcasted_iota(jnp.int32, (128, 64), 1) // RANK).astype(F32)
    for i in range(8):
        f = fields if i == 0 else pltpu.roll(fields, 128 - 16 * i, 1)
        hit0 = jnp.where(f[:, 0:1] == me_f, 1.0, 0.0)
        hit1 = jnp.where(f[:, 1:2] == me_f, 1.0, 0.0)
        p0 = f[:, 3:4] + f[:, 4:5] + f[:, 5:6]
        p1 = f[:, 6:7] + f[:, 7:8] + f[:, 8:9]
        p = hit0 * p0 + hit1 * p1
        mask = jnp.where(f[:, 2:3] == band, 1.0, 0.0) * (hit0 + hit1)
        both = jnp.concatenate([mask, mask * p], axis=1)
        wide = jnp.broadcast_to(p, (128, 128))
        for g in range(8):
            rows = slice((g * 8 + i) * 16, (g * 8 + i) * 16 + 16)
            s["MK"][rows, :] = both[g * 16:g * 16 + 16, :]
            s["PB"][rows, :] = wide[g * 16:g * 16 + 16, :]

    def rows_of(t):
        return pl.ds(pl.multiple_of(t * TILE, TILE), TILE)

    def tile(buf, ck, lo, t):
        return buf[ck, lo * 2 + t // 2, pl.ds((t % 2) * 2, 2)].reshape(TILE, WIDTH)

    for copy in fx:
        copy.wait_recv()
    local_g1.wait()

    for j, (cc, k, lo) in enumerate(use):
        ck = half_of[cc] * 3 + k
        cols = pl.ds(pl.multiple_of(order_b[j] * WIDTH, WIDTH), WIDTH)
        for copy in weight_copies(j):
            copy.wait()

        @pl.loop(0, 4)
        def _(t, ck=ck, lo=lo, cols=cols, j=j):
            rows = rows_of(t)
            xt = tile(X, ck, lo, t)
            ga = dot(xt, s["W"][j % 2, 0])
            up = dot(xt, s["W"][j % 2, 1])
            lr = dot(xt, s["G1T"][:, cols], 1, 1)
            if j == 0:
                s["ACC"][rows, 0:256] = ga
                s["ACC"][rows, 256:512] = up
                s["A64"][rows, :] = lr
            else:
                s["ACC"][rows, 0:256] += ga
                s["ACC"][rows, 256:512] += up
                s["A64"][rows, :] += lr

        if j + 2 < len(use):
            for copy in weight_copies(j + 2):
                copy.start()
        pump(ggens, 1)

    @pl.loop(0, 4)
    def _(t):
        rows = rows_of(t)
        mask = s["MK"][rows, 0:64]
        a = (s["A64"][rows, :] * mask).astype(BF)
        gate = s["ACC"][rows, 0:256] + SCALE * dot(a, l1[...])
        s["ACC"][rows, 0:256] = gate
        s["A"][rows, :] = a
        hid = (gate * jax.nn.sigmoid(gate) * s["ACC"][rows, 256:512]).astype(BF)
        s["HID"][rows, :] = hid
        zp = dot(hid, g2t[...], 1, 1) * mask
        s["ZP"][rows, :] = zp
        s["ZS"][rows, :] = (SCALE * zp).astype(BF)

    local_down.wait()
    local_l2.wait()
    pump(ggens, 1)

    def out_block(dst, cc, k, lo):
        b = lo * 6 + half_of[cc] * 3 + k
        cols = pl.ds(pl.multiple_of(b * WIDTH, WIDTH), WIDTH)

        @pl.loop(0, 4)
        def _(t):
            rows = rows_of(t)
            o = dot(s["HID"][rows, :], s["DOWN"][:, cols]) + dot(s["ZS"][rows, :], s["L2"][:, cols])
            p = s["PB"][rows, :]
            o = o * jnp.concatenate([p, p, p, p], axis=1)
            dst[t // 2, pl.ds((t % 2) * 2, 2)] = o.astype(BF).reshape(2, 8, 16, WIDTH)

    handed = []
    order_k = (2, 1, 0)
    for n, (k, lo) in enumerate([(k, lo) for k in order_k for lo in (0, 1)]):
        slot = s["STAGE"].at[n % 3]
        if n >= 3:
            handed[n - 3].wait_send()
            pending[:] = [copy for copy in pending if copy is not handed[n - 3]]
        out_block(slot, 1, k, lo)
        handed.append(send(slot, SIB.at[k, pl.ds(lo * 2, 2)], sibling))
        out_block(OUT.at[k, pl.ds(lo * 2, 2)], 0, k, lo)
        pump(ggens, 1)
    while ggens:
        pump(ggens, 1)

    def add_block(dst, src, shape):
        lead = shape[:-2]
        total = 1
        for v in lead:
            total *= v
        if total == 1:
            dst[...] = (dst[...].astype(F32) + src[...].astype(F32)).astype(BF)
            return

        @pl.loop(0, total)
        def _(i):
            index = (i,) if len(lead) == 1 else (i // lead[1], i % lead[1])
            dst[index] = (dst[index].astype(F32) + src[index].astype(F32)).astype(BF)

    def reduce_scatter(k, p, me, plus, minus, blk, half):
        _, n, shape, half_shape = RS_PHASES[k][p]
        buf = lambda way, slot: s[("rs", k, p, way, slot)]
        reach = n // 2
        top = around(me, reach, n)
        if half is None:
            up, dn = send(blk(top), buf(0, 0), plus), None
        else:
            up, dn = send(half(top, 0), buf(0, 0), plus), send(half(top, 1), buf(1, 0), minus)
        yield
        for slot, d in enumerate(range(reach - 1, 0, -1)):
            a, b = around(me, d, n), around(me, -d, n)
            begin = slot == 0 and half is not None
            up.wait_recv()
            add_block(half(a, 0) if begin else blk(a), buf(0, slot), half_shape if begin else shape)
            up = send(blk(a), buf(0, slot + 1), plus)
            if dn is not None:
                dn.wait_recv()
                add_block(half(b, 1) if begin else blk(b), buf(1, slot), half_shape if begin else shape)
            dn = send(blk(b), buf(1, slot + 1), minus)
            yield
        up.wait_recv()
        add_block(blk(me), buf(0, reach - 1), shape)
        dn.wait_recv()
        add_block(blk(me), buf(1, reach - 1), shape)

    def scatter_colour(k):
        n0 = order_k.index(k) * 2
        for lo in (0, 1):
            handed[n0 + lo].wait_recv()
            for g in (0, 1):
                add_block(OUT.at[k, lo * 2 + g], SIB.at[k, lo * 2 + g], (4, 8, 16, WIDTH))
        if k == 0:
            views = (
                (lambda i: OUT.at[0, xperm(i)], lambda i, g: OUT.at[0, xperm(i), pl.ds(2 * g, 2)]),
                (lambda i: OUT.at[0, xp, i], lambda i, g: OUT.at[0, xp, i, pl.ds(4 * g, 4)]),
                (lambda i: OUT.at[0, xp, y, i], None),
            )
        elif k == 1:
            views = (
                (lambda i: OUT.at[1, :, i], lambda i, g: OUT.at[1, pl.ds(2 * g, 2), i]),
                (lambda i: OUT.at[1, :, y, i], lambda i, g: OUT.at[1, pl.ds(2 * g, 2), y, i]),
                (lambda i: OUT.at[1, xperm(i), y, z], None),
            )
        else:
            views = (
                (lambda i: OUT.at[2, :, :, i], lambda i, g: OUT.at[2, pl.ds(2 * g, 2), :, i]),
                (lambda i: OUT.at[2, xperm(i), :, z], lambda i, g: OUT.at[2, xperm(i), pl.ds(2 * g, 2), z]),
                (lambda i: OUT.at[2, xp, i, z], None),
            )
        for p, (blk, half) in enumerate(views):
            me, _, plus, minus = steps[RS_PHASES[k][p][0]]
            yield from reduce_scatter(k, p, me, plus, minus, blk, half)

    rgens = [scatter_colour(2), scatter_colour(1), scatter_colour(0)]
    pump(rgens, 1)

    for copy in fg:
        copy.wait_recv()
    for j, (cc, k, lo) in enumerate(use):
        ck = half_of[cc] * 3 + k
        cols = pl.ds(pl.multiple_of(order_b[j] * WIDTH, WIDTH), WIDTH)

        @pl.loop(0, 4)
        def _(t, ck=ck, lo=lo, cols=cols, j=j):
            rows = rows_of(t)
            gt = tile(G, ck, lo, t)
            hg = dot(gt, s["DOWN"][:, cols], 1, 1)
            lr = dot(gt, s["L2"][:, cols], 1, 1)
            if j == 0:
                s["H"][rows, :] = hg
                s["A64"][rows, :] = lr
            else:
                s["H"][rows, :] += hg
                s["A64"][rows, :] += lr

        if j % 3 == 2:
            pump(rgens, 1)

    @pl.loop(0, 4)
    def _(t):
        rows = rows_of(t)
        mask = s["MK"][rows, 0:64]
        cl = (s["A64"][rows, :] * s["MK"][rows, 64:128]).astype(BF)
        s["C"][rows, :] = cl
        p = s["PB"][rows, :]
        dh = s["H"][rows, :] * jnp.concatenate([p, p], axis=1) + SCALE * dot(cl, g2t[...])
        gate = s["ACC"][rows, 0:256]
        sg = jax.nn.sigmoid(gate)
        dg = (dh * s["ACC"][rows, 256:512] * sg * (1.0 + gate * (1.0 - sg))).astype(BF)
        s["DG"][rows, :] = dg
        r = dot(dg, l1[...], 1, 1) * mask
        zr = jnp.concatenate([s["ZP"][rows, :], r], axis=1).T
        z16 = zr[0:16] + zr[16:32] + zr[32:48] + zr[48:64]
        r16 = zr[64:80] + zr[80:96] + zr[96:112] + zr[112:128]
        s["ZR"][t] = jnp.concatenate([z16, r16], axis=0)

    def exchange():
        s["AX"][x] = s["ZR"][x]
        got = [send(s["ZR"].at[around(x, d, 4)], s["AX"].at[x], xdev[d]) for d in (1, 2, 3)]
        yield
        for copy in got:
            copy.wait_recv()
        total = s["AX"][0] + s["AX"][1] + s["AX"][2] + s["AX"][3]
        for q in range(4):
            s["YS"][q] = total[q * 8:q * 8 + 8]
        s["AY"][y] = s["YS"][y]
        got = [send(s["YS"].at[around(y, d, 4)], s["AY"].at[y], ydev[d]) for d in (1, 2, 3)]
        yield
        for copy in got:
            copy.wait_recv()
        s["HS"][...] = s["AY"][0] + s["AY"][1] + s["AY"][2] + s["AY"][3]
        got = send(s["HS"], s["HR"], far)
        yield
        got.wait_recv()
        s["FY"][y] = s["HS"][...] + s["HR"][...]
        got = [send(s["FY"].at[y], s["FY"].at[y], ydev[d]) for d in (1, 2, 3)]
        yield
        for copy in got:
            copy.wait_recv()
        s["FX"][x] = s["FY"][...]
        got = [send(s["FY"], s["FX"].at[x], xdev[d]) for d in (1, 2, 3)]
        yield
        for copy in got:
            copy.wait_recv()

    zgens = [exchange()]
    pump(zgens, 1)
    pump(rgens, 1)
    o_gl[...] = (SCALE * dot(s["A"][...], s["DG"][...], 0, 0)).astype(BF)
    pump(zgens, 1)
    o_dd[...] = (SCALE * dot(s["C"][...], s["HID"][...], 0, 0)).astype(BF)
    pump(rgens, 1)
    while zgens:
        pump(zgens, 1)
        pump(rgens, 1)

    for t in range(4):
        cols = slice(t * TILE, t * TILE + TILE)
        mt = s["MK"][t * TILE:t * TILE + TILE, :].T
        z16 = s["FX"][t, 0:2].reshape(16, TILE)
        r16 = s["FX"][t, 2:4].reshape(16, TILE)
        s["LZ"][:, cols] = (jnp.concatenate([z16] * 4, axis=0) * mt[64:128]).astype(BF)
        full = jnp.concatenate([r16] * 4, axis=0) * mt[0:64]
        top = full.astype(BF)
        s["LR"][0:64, cols] = top
        s["LR"][64:128, cols] = (full - top.astype(F32)).astype(BF)

    for n in range(6):
        for lo in (0, 1):
            cols = slice((lo * 6 + n) * WIDTH, (lo * 6 + n + 1) * WIDTH)
            gt = G[n, lo * 2:lo * 2 + 2].reshape(1024, WIDTH)
            o_dl[:, cols] = (SCALE * dot(s["LZ"][...], gt)).astype(BF)
            xt = X[n, lo * 2:lo * 2 + 2].reshape(1024, WIDTH)
            r = dot(s["LR"][...], xt)
            o_gd[:, cols] = (SCALE * (r[0:64] + r[64:128])).astype(BF)
        pump(rgens, 1)
    while rgens:
        pump(rgens, 1)

    for k in range(3):
        done = OUT[k, xp, y, z].astype(F32)
        for q in range(4):
            s["S32"][q, :, k * WIDTH:(k + 1) * WIDTH] = done[q * 4:q * 4 + 4]
    last = [send(s["S32"].at[g], s["MX"].at[grp], d) for g, d in mates]
    s["MX"][grp] = s["S32"][grp]
    for copy in last:
        copy.wait_recv()
    for q in range(4):
        mixed[:, q * 1536:(q + 1) * 1536] = s["MX"][q].astype(BF)
    for copy in pending:
        copy.wait_send()


def local(tokens, out_grad, routes, tasks, route_probs, gate, up, down, g1, l1, g2, l2):
    probs = []
    for j in range(2):
        p = route_probs[:, j]
        hi = lax.reduce_precision(p, 8, 7)
        mid = lax.reduce_precision(p - hi, 8, 7)
        probs += [hi, mid, p - hi - mid]
    fields = [routes[:, 0].astype(F32), routes[:, 1].astype(F32), tasks.astype(F32)] + probs
    meta = jnp.concatenate([f[:, None] for f in fields] + [jnp.zeros((4, 128 - len(fields)), F32)], axis=1)
    shapes = scratch()
    vmem = pl.BlockSpec(memory_space=pltpu.VMEM)
    hbm = pl.BlockSpec(memory_space=pl.ANY)
    mixed, gd, gl, dd, dl = pl.pallas_call(
        functools.partial(body, tuple(shapes)),
        out_shape=(
            jax.ShapeDtypeStruct((4, 6144), BF),
            jax.ShapeDtypeStruct((64, 6144), BF),
            jax.ShapeDtypeStruct((64, 256), BF),
            jax.ShapeDtypeStruct((64, 256), BF),
            jax.ShapeDtypeStruct((64, 6144), BF),
        ),
        in_specs=[vmem, vmem, vmem, hbm, hbm, hbm, hbm, vmem, vmem, hbm],
        out_specs=(vmem,) * 5,
        scratch_shapes=list(shapes.values()),
        compiler_params=pltpu.CompilerParams(
            collective_id=0, has_side_effects=True, vmem_limit_bytes=64 * 2**20 - 2**18
        ),
        cost_estimate=pl.CostEstimate(flops=24 * 10**9, bytes_accessed=12 * 10**6, transcendentals=10**6),
    )(tokens, out_grad, meta, gate[0], up[0], down[0], g1[0].T, l1[0], g2[0].T, l2[0])
    return mixed, gd.T[None], gl[None], dd.T[None], dl[None]


def solution(mesh):
    rows = P(("dp", "expert", "tensor"), None)
    return jax.shard_map(
        local,
        mesh=mesh,
        in_specs=(
            rows,
            rows,
            rows,
            P(("dp", "expert", "tensor")),
            rows,
            P("expert", None, ("dp", "tensor")),
            P("expert", None, ("dp", "tensor")),
            P("expert", ("dp", "tensor"), None),
            P("expert", None, None),
            P("expert", None, ("dp", "tensor")),
            P("expert", ("dp", "tensor"), None),
            P("expert", None, None),
        ),
        out_specs=(
            rows,
            P("expert", None, None),
            P("expert", None, ("dp", "tensor")),
            P("expert", ("dp", "tensor"), None),
            P("expert", None, None),
        ),
        check_vma=False,
    )
```

time: 645 us -> 214 us (0.33)
  blocking collectives: 381 us -> 0 us
  Pallas kernels: 0 us -> 201 us
  waiting for transfers between devices: 176 us -> 0 us
  matrix products: 47.1 us -> 0 us
  between operations: 14.7 us -> 0.66 us
  starting transfers between devices: 11.4 us -> 0 us
    psum x1 -> x0, blocking collectives: 244 us -> none  [local(): latent_lowrank = lax.psum(z_part, ('dp', 'tensor')).astype(jnp.bfloat16)]
    pallas_call x0 -> x1, Pallas kernels: none -> 201 us  [local(): pl.pallas_call(functools.partial(body, tuple(shapes)), out_shape=(jax.Sha...]
    unnamed x1 -> x0, blocking collectives: 113 us -> none
    all_gather x2 -> x0, waiting for transfers between devices: 107 us -> none  [the longest x1 107 us: local(): lax.all_gather(moved_dout.reshape(slots, width), ('dp', 'tensor'), axis=0...]
    reduce_scatter x1 -> x0, waiting for transfers between devices: 62.4 us -> none  [local(): lax.psum_scatter(jnp.dot(hidden_state, down_w, preferred_element_type=jnp...]
    dot_general x19 -> x0, matrix products: 47.1 us -> none  [the longest x1 6.34 us: local(): jnp.dot(hidden_state, down_w, preferred_element_type=jnp.float32)]
    all_to_all x2 -> x0, blocking collectives: 24.4 us -> none  [the longest x1 13.7 us: local(): lax.all_to_all(send_x.reshape(experts, CAP, width), 'expert', split_axis=...]
    all_to_all x2 -> x0, starting transfers between devices: 11.3 us -> none  [the longest x1 6.18 us: local(): lax.all_to_all(reduced_total.reshape(experts, CAP, width), 'expert', spli...]
  transfers between devices with their start and end apart: 5 -> 0, of which waited for: 4 -> 0; matrix products, arithmetic and copies ran while one was open for 8% -> 0% of each run, Pallas kernels for 0% -> 0%
where the time goes in v1:
time: 214 us
  Pallas kernels  201 us (94%)
  local copies, waits for them, and re-layouts  11 us (5%)
    pallas_call x1, Pallas kernels, local(): pl.pallas_call(functools.partial(body, tuple(shapes)), out_shape=(jax.Sha...  201 us
    unnamed x9, local copies, waits for them, and re-layouts  8.68 us

profile of v1, /device:TPU:1, one launch (start us, length us, event | category | flops | bytes accessed | tf_op | source)
XLA Modules:
  0.0 213.6 jit_solution(1220900393608660431)
XLA Ops:
  0.6 0.7 convert_bitcast_fusion
  1.3 0.8 fusion.1
  2.0 0.8 fusion
  2.8 0.1 copy.25
  2.9 0.1 copy.23
  3.0 0.1 copy.21
  3.1 0.1 copy.24
  3.2 0.1 copy.22
  3.3 0.7 concatenate.3.meta
  4.0 201.3 %shard_map.155 = (bf16[4,6144]{1,0:T(4,128)(2,1)}, bf16[64,6144]{1,0:T(8,128)(2,1)}, bf16[64,256]{1,0:T(8,128)(2,1)}, bf16[64,256]{1,0:T(8,128)(2,1)}, bf16[64,6144]{1,0:T(8,128)(2,1)}) custom-call(bf16[4,6144]{1,0:T(4,128)(2,1)} %tok.1, bf16[4,6144]{1,0:T(4,128)(2,1)} %og.1, f32[4,128]{1,0:T(4,128)} %concatenate.3.meta, bf16[6144,256]{1,0:T(8,128)(2,1)} %bitcast.25, ...), custom_call_target="tpu_custom_call" | custom-call | flops 24000000000 | bytes 12000000 | tf_op jit(solution)/shard_map/pallas_call | solution.py:585
  205.3 1.4 copy.31
  206.7 2.1 copy.32
  208.8 1.4 copy.33
  210.1 1.4 copy.34
  211.5 2.1 copy.35
  (4 shorter events, 0.0 us)

commit v2 on v0

v2 whole, which is shorter than its diff:
```python
import functools

import jax
import jax.numpy as jnp
from jax import lax
from jax.experimental import pallas as pl
from jax.experimental.pallas import tpu as pltpu
from jax.sharding import PartitionSpec as P

RANK = 16
SCALE = 0.5
MESH = pl.DeviceIdType.MESH
BF = jnp.bfloat16
F32 = jnp.float32
WIDTH = 512
TILE = 256
MAX_COPIES = 440

ORDER = (("z", "y", "x"), ("z", "x", "y"), ("y", "x", "z"))
SIZE = {"x": 4, "y": 4, "z": 8}
SUB = ((8, 16, WIDTH), (8, 16, WIDTH), (4, 16, WIDTH))
OFFSETS = {4: (0, -1, 1, 2), 8: (0, -1, 1, -2, 2, -3, 3, 4)}


def rs_buffers():
    shapes = {}
    for k in range(3):
        first, second, third = ORDER[k]
        sub = SUB[k]
        reach = SIZE[third] // 2
        for i, r in enumerate(OFFSETS[SIZE[second]]):
            for d in range(1, reach + 1):
                for sign in "+-":
                    if d < reach or sign == "+-"[i % 2]:
                        shapes[("rs", k, 2, r, sign, d)] = pltpu.VMEM(sub, BF)
        for o in OFFSETS[SIZE[second]][1:]:
            shapes[("rs", k, 1, o)] = pltpu.VMEM(sub, BF)
        for o in OFFSETS[SIZE[first]][1:]:
            shapes[("rs", k, 0, o)] = pltpu.VMEM((16, WIDTH), BF)
    return shapes


class Plan:
    RATE = {"x+": 0.046, "x-": 0.046, "y+": 0.046, "y-": 0.046, "z+": 0.046, "z-": 0.046, "c": 0.4}
    DELAY = 2.5

    def __init__(self):
        self.tasks = []

    def add(self, run, deps=(), cost=0.15, rank=5.0, sends=()):
        task = {"run": run, "deps": list(deps), "cost": cost, "rank": rank, "sends": list(sends)}
        self.tasks.append(task)
        return ("task", len(self.tasks) - 1)

    def order(self):
        when, free, now, done = {}, {}, 0.0, []
        left = list(range(len(self.tasks)))
        while left:
            best = None
            for i in left:
                task = self.tasks[i]
                if any(d not in when for d in task["deps"]):
                    continue
                at = max([when[d] for d in task["deps"]] + [0.0])
                key = (max(at, now), task["rank"], i)
                if best is None or key < best[0]:
                    best = (key, i)
            (begin, _, _), i = best
            task = self.tasks[i]
            now = begin + task["cost"]
            when[("task", i)] = now
            for name, link, size in task["sends"]:
                start = max(now, free.get(link, 0.0))
                free[link] = start + size * 1e-6 / self.RATE[link]
                when[name] = free[link] + self.DELAY
            done.append(i)
            left.remove(i)
        self.length = now
        return done


def scratch():
    shapes = {
        "X": pltpu.VMEM((6, 4, 4, 8, 16, WIDTH), BF),
        "G": pltpu.VMEM((6, 4, 4, 8, 16, WIDTH), BF),
        "OUT": pltpu.VMEM((3, 4, 4, 8, 16, WIDTH), BF),
        "DOWN": pltpu.VMEM((256, 6144), BF),
        "WG": pltpu.VMEM((3, 2, 2, 4, 8, 16, 256), BF),
        "WU": pltpu.VMEM((3, 2, 2, 4, 8, 16, 256), BF),
        "G1T": pltpu.VMEM((64, 6144), BF),
        "L2": pltpu.VMEM((64, 6144), BF),
        "ACC": pltpu.VMEM((1024, 512), F32),
        "A64": pltpu.VMEM((1024, 64), F32),
        "C64": pltpu.VMEM((1024, 64), F32),
        "H": pltpu.VMEM((1024, 256), F32),
        "MK": pltpu.VMEM((1024, 128), F32),
        "PB": pltpu.VMEM((1024, 128), F32),
        "ZP": pltpu.VMEM((1024, 64), F32),
        "HID": pltpu.VMEM((1024, 256), BF),
        "DG": pltpu.VMEM((1024, 256), BF),
        "A": pltpu.VMEM((1024, 64), BF),
        "ZS": pltpu.VMEM((1024, 64), BF),
        "C": pltpu.VMEM((1024, 64), BF),
        "T32": pltpu.VMEM((2, 4, 4, 1536), F32),
        "M32": pltpu.VMEM((4, 128), F32),
        "R": pltpu.VMEM((2, 4, 4, 1536), F32),
        "MR": pltpu.VMEM((4, 4, 128), F32),
        "F": pltpu.VMEM((2, 16, 1536), F32),
        "FM": pltpu.VMEM((16, 128), F32),
        "MZ": pltpu.VMEM((8, 16, 128), BF),
        "MF": pltpu.VMEM((2, 4, 16, 128), BF),
        "ZR": pltpu.VMEM((4, 32, 256), F32),
        "AX": pltpu.VMEM((4, 32, 256), F32),
        "YS": pltpu.VMEM((4, 8, 256), F32),
        "AY": pltpu.VMEM((4, 8, 256), F32),
        "HS": pltpu.VMEM((8, 256), F32),
        "HR": pltpu.VMEM((8, 256), F32),
        "FY": pltpu.VMEM((4, 8, 256), F32),
        "FX": pltpu.VMEM((4, 4, 8, 256), F32),
        "LZ": pltpu.VMEM((64, 1024), BF),
        "LR": pltpu.VMEM((128, 1024), BF),
        "S32": pltpu.VMEM((4, 4, 1536), F32),
        "MX": pltpu.VMEM((4, 4, 1536), F32),
        "send": pltpu.SemaphoreType.DMA((MAX_COPIES,)),
        "recv": pltpu.SemaphoreType.DMA((MAX_COPIES,)),
        "local": pltpu.SemaphoreType.DMA((8,)),
    }
    shapes.update(rs_buffers())
    return shapes


def dot(a, b, ca=1, cb=0):
    return lax.dot_general(a, b, (((ca,), (cb,)), ((), ())), preferred_element_type=F32)


def body(names, tok, og, meta, wg, wu, down, g1t, l1, g2t, l2, mixed, o_gd, o_gl, o_dd, o_dl, *refs):
    s = dict(zip(names, refs))
    X, G, OUT = s["X"], s["G"], s["OUT"]
    dp, ex, x = lax.axis_index("dp"), lax.axis_index("expert"), lax.axis_index("tensor")
    h, y = dp // 4, dp % 4
    zl, c = ex // 2, ex % 2
    z = h * 4 + zl
    xlo, xhi = x % 2, x // 2
    xp = xlo * 2 + xhi
    grp = xlo * 2 + c

    def device(x_, y_, z_, c_):
        return ((z_ // 4) * 4 + y_, (z_ % 4) * 2 + c_, x_)

    def around(v, d, n):
        return lax.rem(v + (d + n), n)

    def xperm(i):
        return lax.rem(i, 2) * 2 + i // 2

    xdev = [device(around(x, d, 4), y, z, c) for d in range(4)]
    ydev = [device(x, around(y, d, 4), z, c) for d in range(4)]
    zdev = {1: device(x, y, around(z, 1, 8), c), -1: device(x, y, around(z, -1, 8), c)}
    far = device(x, y, around(z, 4, 8), c)
    sibling = device(x, y, z, 1 - c)
    xpair = xhi * 2 + (1 - xlo)
    pair = device(xpair, y, z, c)
    pair_sibling = device(xpair, y, z, 1 - c)
    ring = {"x": (x, xdev[1], xdev[3]), "y": (y, ydev[1], ydev[3]), "z": (z, zdev[1], zdev[-1])}
    at_offset = {
        "x": {o: xdev[o % 4] for o in OFFSETS[4]},
        "y": {o: ydev[o % 4] for o in OFFSETS[4]},
        "z": {o: device(x, y, around(z, o, 8), c) for o in OFFSETS[8]},
    }
    plan = Plan()
    copies, waited, pending = {}, set(), []

    def send(name, src, dst, target):
        i = len(copies)
        copy = pltpu.make_async_remote_copy(
            src_ref=src, dst_ref=dst, send_sem=s["send"].at[i], recv_sem=s["recv"].at[i],
            device_id=target, device_id_type=MESH,
        )
        copy.start()
        copies[name] = copy
        pending.append(copy)

    local_down = pltpu.make_async_copy(down, s["DOWN"], s["local"].at[0])
    local_g1 = pltpu.make_async_copy(g1t, s["G1T"], s["local"].at[1])
    local_l2 = pltpu.make_async_copy(l2, s["L2"], s["local"].at[2])

    local_wg = pltpu.make_async_copy(wg, s["WG"], s["local"].at[3])
    local_wu = pltpu.make_async_copy(wu, s["WU"], s["local"].at[4])

    barrier = pltpu.get_barrier_semaphore()
    greeted = xdev[1:] + ydev[1:] + [at_offset["z"][o] for o in OFFSETS[8][1:]] + [sibling, pair_sibling]
    for target in greeted:
        pl.semaphore_signal(barrier, inc=1, device_id=target, device_id_type=MESH)
    local_down.start()
    local_g1.start()
    local_l2.start()
    local_wg.start()
    local_wu.start()
    for q in range(4):
        s["T32"][0, q] = tok[:, q * 1536:(q + 1) * 1536].astype(F32)
        s["T32"][1, q] = og[:, q * 1536:(q + 1) * 1536].astype(F32)
    s["M32"][...] = meta[...].astype(F32)
    pl.semaphore_wait(barrier, len(greeted))

    mates = ((xlo * 2 + 1 - c, sibling), ((1 - xlo) * 2 + c, pair), ((1 - xlo) * 2 + 1 - c, pair_sibling))
    for name, src, dst in (("t0", "T32", "R"), ("m", "M32", "MR"), ("t1", "T32", "R")):
        for i, (g, d) in enumerate(mates):
            if name == "m":
                send((name, i), s["M32"], s["MR"].at[grp], d)
            else:
                a = int(name[1])
                send((name, i), s["T32"].at[a, g], s["R"].at[a, grp], d)
    s["R"][0, grp] = s["T32"][0, grp]
    s["R"][1, grp] = s["T32"][1, grp]
    s["MR"][grp] = s["M32"][...]
    s["ACC"][...] = jnp.zeros((1024, 512), F32)
    s["A64"][...] = jnp.zeros((1024, 64), F32)
    s["C64"][...] = jnp.zeros((1024, 64), F32)
    s["H"][...] = jnp.zeros((1024, 256), F32)
    arrived_first = plan.add(lambda: None, cost=0.0, sends=[((n, i), "c", 1000) for n in ("t0", "m", "t1") for i in range(3)])

    def own_block(a, buf):
        def run():
            for q in range(4):
                s["F"][a, q * 4:q * 4 + 4, :] = s["R"][a, q]
            for k in range(3):
                buf[c * 3 + k, xp, y, z] = s["F"][a, :, k * WIDTH:(k + 1) * WIDTH].astype(BF)

        return plan.add(run, deps=[("t%d" % a, i) for i in range(3)], cost=0.5, rank=1)

    def views(buf, lead, k):
        if k == 0:
            return (
                lambda i: buf.at[lead, xp, y, i],
                lambda i: buf.at[lead, xp, i],
                lambda i2, i1: buf.at[lead, xperm(i2), i1],
            )
        if k == 1:
            return (
                lambda i: buf.at[lead, xp, y, i],
                lambda i: buf.at[lead, xperm(i), y],
                lambda i2, i1: buf.at[lead, xperm(i1), i2],
            )
        return (
            lambda i: buf.at[lead, xp, i, z],
            lambda i: buf.at[lead, xperm(i), :, z],
            lambda i2, i1: buf.at[lead, xperm(i1), :, i2],
        )

    def ring_gather(name, axis, blk, size, dep, via, rank):
        me, plus, minus = ring[axis]
        n = SIZE[axis]
        reach = n // 2
        have = {0: list(dep)}
        for d in range(reach):
            for sign, to in (("+", plus), ("-", minus)):
                if d == reach - 1 and via != sign:
                    continue
                mine = around(me, -d if sign == "+" else d, n)
                deps = dep if d == 0 else [name + (sign, d)]
                key = name + (sign, d + 1)

                def run(key=key, mine=mine, to=to):
                    send(key, blk(mine), blk(mine), to)

                plan.add(run, deps=deps, cost=0.1, rank=rank, sends=[(key, axis + sign, size)])
                have[reach if d == reach - 1 else (-(d + 1) if sign == "+" else d + 1)] = [key]
        return have

    def direct_gather(name, axis, blk, size, dep, rank):
        me, n = ring[axis][0], SIZE[axis]
        have = {0: list(dep)}
        for o in OFFSETS[n][1:]:
            key = name + (o,)

            def run(key=key, o=o):
                send(key, blk(me), blk(me), at_offset[axis][o])

            link = axis + ("+" if o > 0 else "-")
            plan.add(run, deps=dep, cost=0.1, rank=rank, sends=[(key, link, size * abs(o))])
            have[o if 2 * o == n else -o] = [key]
        return have

    def gather(a, buf, k, dep, gate1, gate2, rank):
        ck = c * 3 + k
        axis0, axis1, axis2 = ORDER[k]
        blk0, blk1, sub = views(buf, ck, k)
        piece = 16 * WIDTH * 2
        have0 = direct_gather((a, k, 0), axis0, blk0, piece, dep + gate1, rank)
        dep1 = [d for v in have0.values() for d in v]
        size1 = piece * SIZE[axis0]
        have1 = direct_gather((a, k, 1), axis1, blk1, size1, dep1, rank)
        own, other = {}, {}
        me1, me2, n1, n2 = ring[axis1][0], ring[axis2][0], SIZE[axis1], SIZE[axis2]
        for i, r in enumerate(OFFSETS[n1]):
            i1 = around(me1, r, n1)
            have2 = ring_gather(
                (a, k, 2, r), axis2, lambda i2, i1=i1: sub(i2, i1), size1, have1[r] + gate2, "+-"[i % 2],
                rank + 0.01 * i,
            )
            for o, deps in have2.items():
                own[(r, o)] = deps
                if k < 2:
                    key = ("f", a, k, r, o)

                    def run(key=key, i1=i1, o=o):
                        ref = sub(around(me2, o, n2), i1)
                        send(key, ref, ref, sibling)

                    plan.add(run, deps=deps, cost=0.12, rank=rank + 0.5, sends=[(key, "c", size1)])
                    other[(r, o)] = [key]
        if k == 2:
            for o in OFFSETS[n2]:
                key = ("f", a, k, o)

                def run(key=key, o=o):
                    ref = buf.at[ck, :, :, around(me2, o, n2)]
                    send(key, ref, ref, sibling)

                deps = [d for r in OFFSETS[n1] for d in own[(r, o)]]
                plan.add(run, deps=deps, cost=0.12, rank=rank + 0.5, sends=[(key, "c", size1 * 4)])
                for r in OFFSETS[n1]:
                    other[(r, o)] = [key]
        return own, other

    own_x, own_g = own_block(0, X), own_block(1, G)
    got_x = [gather("x", X, k, [own_x], [], [], 1) for k in range(3)]
    gates = []
    for k in range(3):
        near = [got_x[k][0][(r, o)] for r in OFFSETS[SIZE[ORDER[k][1]]] for o in (-1, 1)]
        gates.append([d for v in near for d in v])
    got_g = [
        gather("g", G, k, [own_g], [], gates[k], 2) for k in range(3)
    ]

    def meta_own():
        for q in range(4):
            s["FM"][q * 4:q * 4 + 4, :] = s["MR"][q]
        s["MZ"][z] = pltpu.roll(s["FM"][...], z * 16, 1).astype(BF)

    def meta_sum():
        total = s["MZ"][0].astype(F32)
        for i in range(1, 8):
            total = total + s["MZ"][i].astype(F32)
        s["MF"][xhi, y] = total.astype(BF)

    t = plan.add(meta_own, deps=[("m", i) for i in range(3)], cost=0.3, rank=3)
    have = direct_gather(("mz",), "z", lambda i: s["MZ"].at[i], 4096, [t], 3)
    t = plan.add(meta_sum, deps=[d for v in have.values() for d in v], cost=0.3, rank=3)
    have = direct_gather(("my",), "y", lambda i: s["MF"].at[xhi, i], 4096, [t], 3)
    t = plan.add(
        lambda: send("mx", s["MF"].at[xhi], s["MF"].at[xhi], xdev[2]),
        deps=[d for v in have.values() for d in v], rank=3, sends=[("mx", "x+", 16384)],
    )

    def masks():
        fields = s["MF"][...].astype(F32).reshape(128, 128)
        me_f = ex.astype(F32)
        band = (lax.broadcasted_iota(jnp.int32, (128, 64), 1) // RANK).astype(F32)
        for i in range(8):
            f = fields if i == 0 else pltpu.roll(fields, 128 - 16 * i, 1)
            hit0 = jnp.where(f[:, 0:1] == me_f, 1.0, 0.0)
            hit1 = jnp.where(f[:, 1:2] == me_f, 1.0, 0.0)
            p0 = f[:, 3:4] + f[:, 4:5] + f[:, 5:6]
            p1 = f[:, 6:7] + f[:, 7:8] + f[:, 8:9]
            p = hit0 * p0 + hit1 * p1
            mask = jnp.where(f[:, 2:3] == band, 1.0, 0.0) * (hit0 + hit1)
            both = jnp.concatenate([mask, mask * p], axis=1)
            wide = jnp.broadcast_to(p, (128, 128))
            for g in range(8):
                rows = slice((g * 8 + i) * 16, (g * 8 + i) * 16 + 16)
                s["MK"][rows, :] = both[g * 16:g * 16 + 16, :]
                s["PB"][rows, :] = wide[g * 16:g * 16 + 16, :]

    masked = plan.add(masks, deps=["mx", t], cost=2.0, rank=6)

    loaded = plan.add(lambda: [copy.wait() for copy in (local_wg, local_wu, local_g1)], cost=0.1, rank=7)
    loaded2 = plan.add(lambda: [copy.wait() for copy in (local_down, local_l2)], cost=0.1, rank=7)
    halves = (c, 1 - c)

    def needed(got, which, k, d):
        found = got[k][which]
        if k == 0:
            keys = [found[(r, d)] for r in OFFSETS[4]]
        else:
            keys = [found[(d, o)] for o in OFFSETS[SIZE[ORDER[k][2]]]]
        return [dep for v in keys for dep in v]

    def block(which, k, d):
        at = around(x, d, 4)
        ck = halves[which] * 3 + k
        rows = pl.ds(pl.multiple_of((at // 2) * 512, 512), 512)
        return ck, xperm(at), lax.rem(at, 2) * 6 + ck, rows

    forward, backward = [], []
    for k in range(3):
        for which in (0, 1):
            for d in OFFSETS[4]:

                def fwd(k=k, which=which, d=d):
                    ck, xi, b, rows = block(which, k, d)

                    @pl.loop(0, 2)
                    def _(i):
                        xt = X[ck, xi, :, :, :, pl.ds(pl.multiple_of(i * 256, 256), 256)].reshape(512, 256)
                        at = (b // 4, (b // 2) % 2, b % 2, pl.ds(i * 2, 2))
                        s["ACC"][rows, 0:256] += dot(xt, s["WG"][at].reshape(256, 256))
                        s["ACC"][rows, 256:512] += dot(xt, s["WU"][at].reshape(256, 256))
                        cols = pl.ds(pl.multiple_of(b * WIDTH + i * 256, 256), 256)
                        s["A64"][rows, :] += dot(xt, s["G1T"][:, cols], 1, 1)

                def bwd(k=k, which=which, d=d):
                    ck, xi, b, rows = block(which, k, d)

                    @pl.loop(0, 2)
                    def _(i):
                        gt = G[ck, xi, :, :, :, pl.ds(pl.multiple_of(i * 256, 256), 256)].reshape(512, 256)
                        cols = pl.ds(pl.multiple_of(b * WIDTH + i * 256, 256), 256)
                        s["H"][rows, :] += dot(gt, s["DOWN"][:, cols], 1, 1)
                        s["C64"][rows, :] += dot(gt, s["L2"][:, cols], 1, 1)

                forward.append(plan.add(fwd, deps=needed(got_x, which, k, d) + [loaded], cost=0.9, rank=10))
                backward.append(plan.add(bwd, deps=needed(got_g, which, k, d) + [loaded2], cost=0.8, rank=20))

    active = []
    for t in range(4):

        def act(t=t):
            rows = slice(t * TILE, t * TILE + TILE)
            mask = s["MK"][rows, 0:64]
            a = (s["A64"][rows, :] * mask).astype(BF)
            gate = s["ACC"][rows, 0:256] + SCALE * dot(a, l1[...])
            s["ACC"][rows, 0:256] = gate
            s["A"][rows, :] = a
            hid = (gate * jax.nn.sigmoid(gate) * s["ACC"][rows, 256:512]).astype(BF)
            s["HID"][rows, :] = hid
            zp = dot(hid, g2t[...], 1, 1) * mask
            s["ZP"][rows, :] = zp
            s["ZS"][rows, :] = (SCALE * zp).astype(BF)

        active.append(plan.add(act, deps=forward + [masked], cost=1.0, rank=11))

    def out_rows(cols, t):
        rows = pl.ds(pl.multiple_of(t * TILE, TILE), TILE)
        o = dot(s["HID"][rows, :], s["DOWN"][:, cols]) + dot(s["ZS"][rows, :], s["L2"][:, cols])
        p = s["PB"][rows, :]
        return o * jnp.concatenate([p, p, p, p], axis=1)

    order_k = (2, 0, 1)
    out_of = {}
    for n, (k, lo) in enumerate([(k, lo) for k in order_k for lo in (0, 1)]):

        def theirs(n=n, k=k, lo=lo):
            b = lo * 6 + halves[1] * 3 + k
            cols = pl.ds(pl.multiple_of(b * WIDTH, WIDTH), WIDTH)

            stage = s["WG" if n < 3 else "WU"].at[n % 3]

            @pl.loop(0, 4)
            def _(t):
                o = out_rows(cols, t).astype(BF)
                for f in (0, 1):
                    half = o[:, f * 256:f * 256 + 256].reshape(2, 8, 16, 256)
                    stage[f, t // 2, pl.ds((t % 2) * 2, 2)] = half

            for f in (0, 1):
                dst = OUT.at[k, pl.ds(lo * 2, 2), :, :, :, pl.ds(f * 256, 256)]
                send(("o", k, lo, f), stage.at[f], dst, sibling)

        plan.add(
            theirs, deps=active + [loaded2], cost=1.6, rank=12 + 0.1 * n,
            sends=[(("o", k, lo, f), "c", 2**19) for f in (0, 1)],
        )

    for n, (k, lo) in enumerate([(k, lo) for k in order_k for lo in (0, 1)]):

        def ours(n=n, k=k, lo=lo):
            b = lo * 6 + halves[0] * 3 + k
            cols = pl.ds(pl.multiple_of(b * WIDTH, WIDTH), WIDTH)

            @pl.loop(0, 4)
            def _(t):
                at = (k, lo * 2 + t // 2, pl.ds((t % 2) * 2, 2))
                o = out_rows(cols, t) + OUT[at].reshape(TILE, WIDTH).astype(F32)
                OUT[at] = o.astype(BF).reshape(2, 8, 16, WIDTH)

        out_of[(k, lo)] = plan.add(ours, deps=active + [("o", k, lo, f) for f in (0, 1)], cost=1.6, rank=13 + 0.1 * n)

    def add_block(dst, sources, shape):
        part = shape[0] if len(shape) == 2 else min(4, shape[0])
        for i in range(0, shape[0], part):
            at = pl.ds(i, part)
            total = dst[at].astype(F32)
            for src in sources:
                total = total + src[at].astype(F32)
            dst[at] = total.astype(BF)

    def ring_reduce(name, axis, blk, shape, dep, via, rank):
        me, plus, minus = ring[axis]
        n = SIZE[axis]
        reach = n // 2
        size = 2
        for v in shape:
            size *= v
        chain = {}
        for d in range(reach, 0, -1):
            for sign, to in (("+", plus), ("-", minus)):
                if d == reach and sign != via:
                    continue
                at = around(me, d if sign == "+" else -d, n)
                key = name + (sign, d)
                before = chain.get(sign)

                def run(key=key, at=at, to=to, before=before):
                    if before is not None:
                        add_block(blk(at), [s[before]], shape)
                    send(key, blk(at), s[key], to)

                deps = list(dep) + ([before] if before is not None else [])
                cost = 0.1 if before is None else 0.35
                plan.add(run, deps=deps, rank=rank, cost=cost, sends=[(key, axis + sign, size)])
                chain[sign] = key

        def finish():
            add_block(blk(me), [s[chain[sign]] for sign in "+-"], shape)

        return plan.add(finish, deps=list(dep) + [chain["+"], chain["-"]], cost=0.4, rank=rank)

    def direct_reduce(name, axis, blk, shape, dep, rank):
        me, n = ring[axis][0], SIZE[axis]
        size = 2
        for v in shape:
            size *= v
        keys = []
        for o in sorted(OFFSETS[n][1:], key=lambda o: -abs(o)):
            key = name + (o,)

            def run(key=key, o=o):
                send(key, blk(around(me, o, n)), s[key], at_offset[axis][o])

            link = axis + ("+" if o > 0 else "-")
            plan.add(run, deps=dep(o), rank=rank, cost=0.1, sends=[(key, link, size * abs(o))])
            keys.append(key)

        def finish():
            add_block(blk(me), [s[key] for key in keys], shape)

        return plan.add(finish, deps=dep(0) + keys, cost=0.4, rank=rank)

    def scatter(k):
        axis0, axis1, axis2 = ORDER[k]
        blk0, blk1, sub = views(OUT, k, k)
        ready = [out_of[(k, 0)], out_of[(k, 1)]]
        me1, n1 = ring[axis1][0], SIZE[axis1]
        parts = {}
        for i, r in enumerate(OFFSETS[n1]):
            i1 = around(me1, r, n1)
            parts[r] = ring_reduce(
                ("rs", k, 2, r), axis2, lambda i2, i1=i1: sub(i2, i1), SUB[k], ready, "+-"[i % 2],
                4 - 0.1 * i,
            )
        one = direct_reduce(("rs", k, 1), axis1, blk1, SUB[k], lambda o: [parts[o]], 3)
        return direct_reduce(("rs", k, 0), axis0, blk0, (16, WIDTH), lambda o: [one], 2)

    summed = [scatter(k) for k in order_k]

    reverse = []
    for t in range(4):

        def deact(t=t):
            rows = slice(t * TILE, t * TILE + TILE)
            mask = s["MK"][rows, 0:64]
            cl = (s["C64"][rows, :] * s["MK"][rows, 64:128]).astype(BF)
            s["C"][rows, :] = cl
            p = s["PB"][rows, :]
            dh = s["H"][rows, :] * jnp.concatenate([p, p], axis=1) + SCALE * dot(cl, g2t[...])
            gate = s["ACC"][rows, 0:256]
            sg = jax.nn.sigmoid(gate)
            dg = (dh * s["ACC"][rows, 256:512] * sg * (1.0 + gate * (1.0 - sg))).astype(BF)
            s["DG"][rows, :] = dg
            r = dot(dg, l1[...], 1, 1) * mask
            zr = jnp.concatenate([s["ZP"][rows, :], r], axis=1).T
            z16 = zr[0:16] + zr[16:32] + zr[32:48] + zr[48:64]
            r16 = zr[64:80] + zr[80:96] + zr[96:112] + zr[112:128]
            s["ZR"][t] = jnp.concatenate([z16, r16], axis=0)

        reverse.append(plan.add(deact, deps=backward + active, cost=1.3, rank=21))

    def ex1():
        s["AX"][x] = s["ZR"][x]
        for d in (1, 2, 3):
            send(("e1", d), s["ZR"].at[around(x, d, 4)], s["AX"].at[x], xdev[d])

    def ex2():
        total = s["AX"][0] + s["AX"][1] + s["AX"][2] + s["AX"][3]
        for q in range(4):
            s["YS"][q] = total[q * 8:q * 8 + 8]
        s["AY"][y] = s["YS"][y]
        for d in (1, 2, 3):
            send(("e2", d), s["YS"].at[around(y, d, 4)], s["AY"].at[y], ydev[d])

    def ex3():
        s["HS"][...] = s["AY"][0] + s["AY"][1] + s["AY"][2] + s["AY"][3]
        send(("e3", 1), s["HS"], s["HR"], far)

    def ex4():
        s["FY"][y] = s["HS"][...] + s["HR"][...]
        for d in (1, 2, 3):
            send(("e4", d), s["FY"].at[y], s["FY"].at[y], ydev[d])

    def ex5():
        s["FX"][x] = s["FY"][...]
        for d in (1, 2, 3):
            send(("e5", d), s["FY"], s["FX"].at[x], xdev[d])

    deps = reverse
    for n, (run, axis, size) in enumerate(((ex1, "x", 32768), (ex2, "y", 8192), (ex3, "z", 32768), (ex4, "y", 8192), (ex5, "x", 32768))):
        names = [("e%d" % (n + 1), d) for d in ((1,) if n == 2 else (1, 2, 3))]
        plan.add(run, deps=deps, cost=0.4, rank=0.5, sends=[(m, axis + "+-"[i % 2], size) for i, m in enumerate(names)])
        deps = names

    def lowrank():
        o_gl[...] = (SCALE * dot(s["A"][...], s["DG"][...], 0, 0)).astype(BF)
        o_dd[...] = (SCALE * dot(s["C"][...], s["HID"][...], 0, 0)).astype(BF)

    plan.add(lowrank, deps=reverse, cost=2.0, rank=23)

    def left_sides():
        for t in range(4):
            cols = slice(t * TILE, t * TILE + TILE)
            mt = s["MK"][t * TILE:t * TILE + TILE, :].T
            z16 = s["FX"][t, 0:2].reshape(16, TILE)
            r16 = s["FX"][t, 2:4].reshape(16, TILE)
            s["LZ"][:, cols] = (jnp.concatenate([z16] * 4, axis=0) * mt[64:128]).astype(BF)
            full = jnp.concatenate([r16] * 4, axis=0) * mt[0:64]
            top = full.astype(BF)
            s["LR"][0:64, cols] = top
            s["LR"][64:128, cols] = (full - top.astype(F32)).astype(BF)

    left = plan.add(left_sides, deps=deps, cost=1.5, rank=22)
    for n in range(4):

        def grads(n=n):
            @pl.loop(3 * n, 3 * n + 3)
            def _(b):
                cols = pl.ds(pl.multiple_of(b * WIDTH, WIDTH), WIDTH)
                at = (b % 6, pl.ds((b // 6) * 2, 2))
                o_dl[:, cols] = (SCALE * dot(s["LZ"][...], G[at].reshape(1024, WIDTH))).astype(BF)
                r = dot(s["LR"][...], X[at].reshape(1024, WIDTH))
                o_gd[:, cols] = (SCALE * (r[0:64] + r[64:128])).astype(BF)

        plan.add(grads, deps=[left], cost=2.7, rank=24)

    def give_back():
        for k in range(3):
            done = OUT[k, xp, y, z].astype(F32)
            for q in range(4):
                s["S32"][q, :, k * WIDTH:(k + 1) * WIDTH] = done[q * 4:q * 4 + 4]
        for i, (g, d) in enumerate(mates):
            send(("l", i), s["S32"].at[g], s["MX"].at[grp], d)
        s["MX"][grp] = s["S32"][grp]

    plan.add(give_back, deps=summed, cost=0.5, rank=0, sends=[(("l", i), "c", 24576) for i in range(3)])

    def finish():
        for q in range(4):
            mixed[:, q * 1536:(q + 1) * 1536] = s["MX"][q].astype(BF)

    plan.add(finish, deps=[("l", i) for i in range(3)], cost=0.3, rank=0)

    for i in plan.order():
        task = plan.tasks[i]
        for d in task["deps"]:
            if d in copies and d not in waited:
                copies[d].wait_recv()
                waited.add(d)
        task["run"]()
    for d in copies:
        if d not in waited:
            copies[d].wait_recv()
    for copy in pending:
        copy.wait_send()


def hand_over(*refs):
    for src, dst in zip(refs[:5], refs[5:]):
        dst[...] = src[...]


def local(tokens, out_grad, routes, tasks, route_probs, gate, up, down, g1, l1, g2, l2):
    probs = []
    for j in range(2):
        p = route_probs[:, j]
        hi = lax.reduce_precision(p, 8, 7)
        mid = lax.reduce_precision(p - hi, 8, 7)
        probs += [hi, mid, p - hi - mid]
    fields = [routes[:, 0].astype(F32), routes[:, 1].astype(F32), tasks.astype(F32)] + probs
    meta = jnp.concatenate([f[:, None] for f in fields] + [jnp.zeros((4, 128 - len(fields)), F32)], axis=1)
    shapes = scratch()
    shapes_out = tuple(
        jax.ShapeDtypeStruct(v, BF) for v in ((4, 6144), (64, 6144), (64, 256), (64, 256), (64, 6144))
    )
    w_shape = (3, 2, 2, 4, 8, 16, 256)
    vmem = pl.BlockSpec(memory_space=pltpu.VMEM)
    hbm = pl.BlockSpec(memory_space=pl.ANY)
    mixed, gd, gl, dd, dl = pl.pallas_call(
        functools.partial(body, tuple(shapes)),
        out_shape=shapes_out,
        in_specs=[vmem, vmem, vmem, hbm, hbm, hbm, hbm, vmem, vmem, hbm],
        out_specs=(vmem,) * 5,
        scratch_shapes=list(shapes.values()),
        compiler_params=pltpu.CompilerParams(
            collective_id=0, has_side_effects=True, vmem_limit_bytes=64 * 2**20 - 2**18
        ),
        cost_estimate=pl.CostEstimate(flops=24 * 10**9, bytes_accessed=12 * 10**6, transcendentals=10**6),
    )(tokens, out_grad, meta, gate.reshape(w_shape), up.reshape(w_shape), down[0], g1[0].T, l1[0], g2[0].T, l2[0])
    mixed, gd, gl, dd, dl = pl.pallas_call(
        hand_over, out_shape=shapes_out, in_specs=[vmem] * 5, out_specs=(vmem,) * 5,
    )(mixed, gd, gl, dd, dl)
    return mixed, gd.T[None], gl[None], dd.T[None], dl[None]


def solution(mesh):
    rows = P(("dp", "expert", "tensor"), None)
    return jax.shard_map(
        local,
        mesh=mesh,
        in_specs=(
            rows,
            rows,
            rows,
            P(("dp", "expert", "tensor")),
            rows,
            P("expert", None, ("dp", "tensor")),
            P("expert", None, ("dp", "tensor")),
            P("expert", ("dp", "tensor"), None),
            P("expert", None, None),
            P("expert", None, ("dp", "tensor")),
            P("expert", ("dp", "tensor"), None),
            P("expert", None, None),
        ),
        out_specs=(
            rows,
            P("expert", None, None),
            P("expert", None, ("dp", "tensor")),
            P("expert", ("dp", "tensor"), None),
            P("expert", None, None),
        ),
        check_vma=False,
    )
```

time: 645 us -> 178 us (0.28)
  blocking collectives: 381 us -> 0 us
  waiting for transfers between devices: 176 us -> 0 us
  Pallas kernels: 0 us -> 172 us
  matrix products: 47.1 us -> 0 us
  between operations: 14.7 us -> 0.65 us
  starting transfers between devices: 11.4 us -> 0 us
  local copies, waits for them, and re-layouts: 11.6 us -> 2.65 us
    psum x1 -> x0, blocking collectives: 244 us -> none  [local(): latent_lowrank = lax.psum(z_part, ('dp', 'tensor')).astype(jnp.bfloat16)]
    pallas_call x0 -> x2, Pallas kernels: none -> 172 us  [the longest x1 169 us: local(): pl.pallas_call(functools.partial(body, tuple(shapes)), out_shape=shapes_o...]
    unnamed x1 -> x0, blocking collectives: 113 us -> none
    all_gather x2 -> x0, waiting for transfers between devices: 107 us -> none  [the longest x1 107 us: local(): lax.all_gather(moved_dout.reshape(slots, width), ('dp', 'tensor'), axis=0...]
    reduce_scatter x1 -> x0, waiting for transfers between devices: 62.4 us -> none  [local(): lax.psum_scatter(jnp.dot(hidden_state, down_w, preferred_element_type=jnp...]
    dot_general x19 -> x0, matrix products: 47.1 us -> none  [the longest x1 6.34 us: local(): jnp.dot(hidden_state, down_w, preferred_element_type=jnp.float32)]
    all_to_all x2 -> x0, blocking collectives: 24.4 us -> none  [the longest x1 13.7 us: local(): lax.all_to_all(send_x.reshape(experts, CAP, width), 'expert', split_axis=...]
    all_to_all x2 -> x0, starting transfers between devices: 11.3 us -> none  [the longest x1 6.18 us: local(): lax.all_to_all(reduced_total.reshape(experts, CAP, width), 'expert', spli...]
  transfers between devices with their start and end apart: 5 -> 0, of which waited for: 4 -> 0; matrix products, arithmetic and copies ran while one was open for 8% -> 0% of each run, Pallas kernels for 0% -> 0%
where the time goes in v2:
time: 178 us; the launch traced here: 176 us
  Pallas kernels  172 us (97%)
  local copies, waits for them, and re-layouts  2.65 us (1%)
    pallas_call x1, Pallas kernels, local(): pl.pallas_call(functools.partial(body, tuple(shapes)), out_shape=shapes_o...  169 us

profile of v2, /device:TPU:1, one launch (start us, length us, event | category | flops | bytes accessed | tf_op | source)
XLA Modules:
  0.0 175.7 jit_solution(11810885082054598405)
XLA Ops:
  0.6 0.7 convert_bitcast_fusion
  1.3 0.8 fusion.1
  2.0 0.8 fusion
  2.8 0.1 copy.25
  2.9 0.1 copy.23
  3.0 0.1 copy.21
  3.1 0.1 copy.24
  3.2 0.1 copy.22
  3.3 0.7 concatenate.3.meta
  4.0 169.1 %shard_map.155 = (bf16[4,6144]{1,0:T(4,128)(2,1)}, bf16[64,6144]{1,0:T(8,128)(2,1)}, bf16[64,256]{1,0:T(8,128)(2,1)}, bf16[64,256]{1,0:T(8,128)(2,1)}, bf16[64,6144]{1,0:T(8,128)(2,1)}) custom-call(bf16[4,6144]{1,0:T(4,128)(2,1)} %tok.1, bf16[4,6144]{1,0:T(4,128)(2,1)} %og.1, f32[4,128]{1,0:T(4,128)} %concatenate.3.meta, ...), custom_call_target="tpu_custom_call" | custom-call | flops 24000000000 | bytes 12000000 | tf_op jit(solution)/shard_map/pallas_call | solution.py:706
  173.0 2.6 %shard_map.156 = (bf16[4,6144]{1,0:T(4,128)(2,1)}, bf16[64,6144]{1,0:T(8,128)(2,1)}, bf16[64,256]{1,0:T(8,128)(2,1)}, bf16[64,256]{1,0:T(8,128)(2,1)}, bf16[64,6144]{1,0:T(8,128)(2,1)}) custom-call(bf16[4,6144]{1,0:T(4,128)(2,1)} %get-tuple-element.15.refs_0_, bf16[64,6144]{1,0:T(8,128)(2,1)} %get-tuple-element.16.refs_1_, ...), custom_call_target="tpu_custom_call" | custom-call | tf_op jit(solution)/shard_map/pallas_call | solution.py:717
  (4 shorter events, 0.0 us)

commit v3 on v2

--- a/solution.py
+++ b/solution.py
@@ -41,8 +41,8 @@
 
 
 class Plan:
-    RATE = {"x+": 0.046, "x-": 0.046, "y+": 0.046, "y-": 0.046, "z+": 0.046, "z-": 0.046, "c": 0.4}
-    DELAY = 2.5
+    RATE = {"x+": 0.046, "x-": 0.046, "y+": 0.046, "y-": 0.046, "z+": 0.04, "z-": 0.04, "c": 0.4}
+    DELAY = 2.8
 
     def __init__(self):
         self.tasks = []
@@ -263,7 +263,7 @@
                 def run(key=key, mine=mine, to=to):
                     send(key, blk(mine), blk(mine), to)
 
-                plan.add(run, deps=deps, cost=0.1, rank=rank, sends=[(key, axis + sign, size)])
+                plan.add(run, deps=deps, cost=0.15, rank=rank, sends=[(key, axis + sign, size)])
                 have[reach if d == reach - 1 else (-(d + 1) if sign == "+" else d + 1)] = [key]
         return have
 
@@ -277,7 +277,7 @@
                 send(key, blk(me), blk(me), at_offset[axis][o])
 
             link = axis + ("+" if o > 0 else "-")
-            plan.add(run, deps=dep, cost=0.1, rank=rank, sends=[(key, link, size * abs(o))])
+            plan.add(run, deps=dep, cost=0.15, rank=rank, sends=[(key, link, size * abs(o))])
             have[o if 2 * o == n else -o] = [key]
         return have
 
@@ -300,27 +300,18 @@
             )
             for o, deps in have2.items():
                 own[(r, o)] = deps
-                if k < 2:
-                    key = ("f", a, k, r, o)
-
-                    def run(key=key, i1=i1, o=o):
-                        ref = sub(around(me2, o, n2), i1)
-                        send(key, ref, ref, sibling)
-
-                    plan.add(run, deps=deps, cost=0.12, rank=rank + 0.5, sends=[(key, "c", size1)])
-                    other[(r, o)] = [key]
-        if k == 2:
-            for o in OFFSETS[n2]:
-                key = ("f", a, k, o)
-
-                def run(key=key, o=o):
-                    ref = buf.at[ck, :, :, around(me2, o, n2)]
-                    send(key, ref, ref, sibling)
-
-                deps = [d for r in OFFSETS[n1] for d in own[(r, o)]]
-                plan.add(run, deps=deps, cost=0.12, rank=rank + 0.5, sends=[(key, "c", size1 * 4)])
-                for r in OFFSETS[n1]:
-                    other[(r, o)] = [key]
+        for o in OFFSETS[n2]:
+            key = ("f", a, k, o)
+
+            def run(key=key, o=o):
+                i2 = around(me2, o, n2)
+                ref = buf.at[ck, xperm(i2)] if k == 0 else buf.at[ck, :, i2] if k == 1 else buf.at[ck, :, :, i2]
+                send(key, ref, ref, sibling)
+
+            deps = [d for r in OFFSETS[n1] for d in own[(r, o)]]
+            plan.add(run, deps=deps, cost=0.15, rank=rank + 0.5, sends=[(key, "c", size1 * 4)])
+            for r in OFFSETS[n1]:
+                other[(r, o)] = [key]
         return own, other
 
     own_x, own_g = own_block(0, X), own_block(1, G)
@@ -484,7 +475,7 @@
                 o = out_rows(cols, t) + OUT[at].reshape(TILE, WIDTH).astype(F32)
                 OUT[at] = o.astype(BF).reshape(2, 8, 16, WIDTH)
 
-        out_of[(k, lo)] = plan.add(ours, deps=active + [("o", k, lo, f) for f in (0, 1)], cost=1.6, rank=13 + 0.1 * n)
+        out_of[(k, lo)] = plan.add(ours, deps=active + [("o", k, lo, f) for f in (0, 1)], cost=1.6, rank=12.32 + 0.05 * n)
 
     def add_block(dst, sources, shape):
         part = shape[0] if len(shape) == 2 else min(4, shape[0])
@@ -517,7 +508,7 @@
                     send(key, blk(at), s[key], to)
 
                 deps = list(dep) + ([before] if before is not None else [])
-                cost = 0.1 if before is None else 0.35
+                cost = 0.15 if before is None else 0.5
                 plan.add(run, deps=deps, rank=rank, cost=cost, sends=[(key, axis + sign, size)])
                 chain[sign] = key
 

time: 178 us -> 172 us (0.966)
  Pallas kernels: 172 us -> 166 us
    pallas_call x1, Pallas kernels: 169 us -> 163 us  [local(): pl.pallas_call(functools.partial(body, tuple(shapes)), out_shape=shapes_o...]
where the time goes in v3:
time: 172 us; the launch traced here: 170 us
  Pallas kernels  166 us (97%)
  local copies, waits for them, and re-layouts  2.65 us (2%)
    pallas_call x1, Pallas kernels, local(): pl.pallas_call(functools.partial(body, tuple(shapes)), out_shape=shapes_o...  163 us

profile of v3, /device:TPU:1, one launch (start us, length us, event | category | flops | bytes accessed | tf_op | source)
XLA Modules:
  0.0 169.7 jit_solution(12303223746400977331)
XLA Ops:
  0.6 0.7 convert_bitcast_fusion
  1.3 0.8 fusion.1
  2.0 0.8 fusion
  2.8 0.1 copy.25
  2.9 0.1 copy.23
  3.0 0.1 copy.21
  3.1 0.1 copy.24
  3.2 0.1 copy.22
  3.3 0.7 concatenate.3.meta
  4.0 163.0 %shard_map.155 = (bf16[4,6144]{1,0:T(4,128)(2,1)}, bf16[64,6144]{1,0:T(8,128)(2,1)}, bf16[64,256]{1,0:T(8,128)(2,1)}, bf16[64,256]{1,0:T(8,128)(2,1)}, bf16[64,6144]{1,0:T(8,128)(2,1)}) custom-call(bf16[4,6144]{1,0:T(4,128)(2,1)} %tok.1, bf16[4,6144]{1,0:T(4,128)(2,1)} %og.1, f32[4,128]{1,0:T(4,128)} %concatenate.3.meta, ...), custom_call_target="tpu_custom_call" | custom-call | flops 24000000000 | bytes 12000000 | tf_op jit(solution)/shard_map/pallas_call | solution.py:697
  167.0 2.6 %shard_map.156 = (bf16[4,6144]{1,0:T(4,128)(2,1)}, bf16[64,6144]{1,0:T(8,128)(2,1)}, bf16[64,256]{1,0:T(8,128)(2,1)}, bf16[64,256]{1,0:T(8,128)(2,1)}, bf16[64,6144]{1,0:T(8,128)(2,1)}) custom-call(bf16[4,6144]{1,0:T(4,128)(2,1)} %get-tuple-element.15.refs_0_, bf16[64,6144]{1,0:T(8,128)(2,1)} %get-tuple-element.16.refs_1_, ...), custom_call_target="tpu_custom_call" | custom-call | tf_op jit(solution)/shard_map/pallas_call | solution.py:708
  (4 shorter events, 0.0 us)

commit v4 on v3

--- a/solution.py
+++ b/solution.py
@@ -2,6 +2,7 @@
 
 import jax
 import jax.numpy as jnp
+import numpy as np
 from jax import lax
 from jax.experimental import pallas as pl
 from jax.experimental.pallas import tpu as pltpu
@@ -410,8 +411,8 @@
                         s["H"][rows, :] += dot(gt, s["DOWN"][:, cols], 1, 1)
                         s["C64"][rows, :] += dot(gt, s["L2"][:, cols], 1, 1)
 
-                forward.append(plan.add(fwd, deps=needed(got_x, which, k, d) + [loaded], cost=0.9, rank=10))
-                backward.append(plan.add(bwd, deps=needed(got_g, which, k, d) + [loaded2], cost=0.8, rank=20))
+                forward.append(plan.add(fwd, deps=needed(got_x, which, k, d) + [loaded], cost=0.7, rank=10))
+                backward.append(plan.add(bwd, deps=needed(got_g, which, k, d) + [loaded2], cost=0.6, rank=20))
 
     active = []
     for t in range(4):
@@ -686,7 +687,8 @@
         mid = lax.reduce_precision(p - hi, 8, 7)
         probs += [hi, mid, p - hi - mid]
     fields = [routes[:, 0].astype(F32), routes[:, 1].astype(F32), tasks.astype(F32)] + probs
-    meta = jnp.concatenate([f[:, None] for f in fields] + [jnp.zeros((4, 128 - len(fields)), F32)], axis=1)
+    lanes = np.eye(len(fields), 128, dtype=np.float32)
+    meta = sum(f[:, None] * lanes[i][None, :] for i, f in enumerate(fields))
     shapes = scratch()
     shapes_out = tuple(
         jax.ShapeDtypeStruct(v, BF) for v in ((4, 6144), (64, 6144), (64, 256), (64, 256), (64, 6144))

time: 172 us -> 170 us (0.988)
  other arithmetic: 0.68 us -> 3.62 us
  local copies, waits for them, and re-layouts: 2.65 us -> 0 us
  Pallas kernels: 166 us -> 164 us
where the time goes in v4:
time: 170 us; the launch traced here: 169 us
  Pallas kernels  164 us (96%)
  other arithmetic  3.62 us (2%)
    pallas_call x1, Pallas kernels, local(): pl.pallas_call(functools.partial(body, tuple(shapes)), out_shape=shapes_o...  162 us

profile of v4, /device:TPU:1, one launch (start us, length us, event | category | flops | bytes accessed | tf_op | source)
XLA Modules:
  0.0 168.5 jit_solution(4331119228628269964)
XLA Ops:
  0.6 0.7 convert_element_type.13
  1.3 0.8 convert_bitcast_fusion.1
  2.0 0.8 reduce-precision_bitcast_fusion.3
  2.8 1.4 multiply_add_fusion.meta
  4.3 161.6 %shard_map.236 = (bf16[4,6144]{1,0:T(4,128)(2,1)}, bf16[64,6144]{1,0:T(8,128)(2,1)}, bf16[64,256]{1,0:T(8,128)(2,1)}, bf16[64,256]{1,0:T(8,128)(2,1)}, bf16[64,6144]{1,0:T(8,128)(2,1)}) custom-call(bf16[4,6144]{1,0:T(4,128)(2,1)} %tok.1, bf16[4,6144]{1,0:T(4,128)(2,1)} %og.1, f32[4,128]{1,0:T(4,128)} %multiply_add_fusion.meta, ...), custom_call_target="tpu_custom_call" | custom-call | flops 24000000000 | bytes 12000000 | tf_op jit(solution)/shard_map/pallas_call | solution.py:699
  165.9 2.6 %shard_map.237 = (bf16[4,6144]{1,0:T(4,128)(2,1)}, bf16[64,6144]{1,0:T(8,128)(2,1)}, bf16[64,256]{1,0:T(8,128)(2,1)}, bf16[64,256]{1,0:T(8,128)(2,1)}, bf16[64,6144]{1,0:T(8,128)(2,1)}) custom-call(bf16[4,6144]{1,0:T(4,128)(2,1)} %get-tuple-element.15.refs_0_, bf16[64,6144]{1,0:T(8,128)(2,1)} %get-tuple-element.16.refs_1_, ...), custom_call_target="tpu_custom_call" | custom-call | tf_op jit(solution)/shard_map/pallas_call | solution.py:710
